TPU v7x, 256 devices: a whole 4x4x8 slice. The times are simulated.
256 devices in a mesh: group: 8 (over z), member: 32 (over y, x, core).
Axes of the slice: x: 4, y: 4, z: 8, core: 2. Of those that a mesh axis runs over, the one named last changes fastest.
Arguments:
- patterns: float32 [256, 2, 256, 512], P('group', None, 'member'), may hold values from -6 to 6
- operators: float32 [100, 2, 256, 512], P(None, None, 'member'), may hold values from -1 to 1
- partners: int32 [256, 8], P('group'), may hold values from 0 to 255, as said below
- operator_index: int32 [256, 8], P('group'), may hold values from 0 to 99
- child_parent: int32 [512], P('group'), may hold values from 0 to 255, as said below
- child_octant: int32 [512], P('group'), may hold values from 0 to 7, as said below
Outputs:
- child_patterns: float32 [512, 2, 128, 256], P('group', None, 'member')
Inputs may be any that keep to these rules, and one draw needn't show every extreme that they name: `partners`: an entry of cluster c's list lies in c's own group block (clusters g * 32 to (g + 1) * 32 - 1); only the first 8 clusters of a block may also name any of the last 8 clusters of the previous block, and only the last 8 clusters any of the first 8 clusters of the next block. `child_parent`: the parent of a child in child block g (children g * 64 to (g + 1) * 64 - 1) lies in cluster block g; every cluster has at least one child; every cluster has 1 to 3 children, and in every block some cluster has exactly 3. `child_octant`: children of one parent have different octants.
All inputs are finite; a program needn't handle non-finite values.
Results may differ from a plain program's by a relative error of at most 0.0003.
Values sent between devices are 32-bit elements; how exact they have to be, the bound alone decides.
A program may use at most 64 MiB of HBM per device.

v0:
```python
import math

import jax
import jax.numpy as jnp
from jax import lax
from jax.sharding import Mesh
from jax.sharding import PartitionSpec as P

NTC = 128
NPC = 256
MEMBER = ("member_0", "member_1", "member_2")


shift_reach = 6.0


def with_halo(cells, sides, width):
    for axis, dim in sides:
        count = lax.axis_size(axis)
        ends = count - 1
        head = lax.slice_in_dim(cells, 0, width, axis=dim)
        tail = lax.slice_in_dim(cells, cells.shape[dim] - width, cells.shape[dim], axis=dim)
        cells = jnp.concatenate(
            [
                lax.ppermute(tail, axis, [(i, (i + 1) % count) for i in range(ends)]),
                cells,
                lax.ppermute(head, axis, [((i + 1) % count, i) for i in range(ends)]),
            ],
            axis=dim,
        )
    return cells


def split_up(shard, dim, devices):
    lengths = shard.shape
    pieces = shard.reshape(*lengths[:dim], devices, lengths[dim] // devices, *lengths[dim + 1 :])
    return jnp.moveaxis(pieces, dim, 0)


def in_order(pieces, dim):
    lengths = list(pieces.shape[1:])
    lengths[dim] *= pieces.shape[0]
    return jnp.moveaxis(pieces, 0, dim).reshape(lengths)


def turned_blocks(pieces, axes, order):
    lengths = [lax.axis_size(a) for a in axes]
    pieces = pieces.reshape(*lengths, *pieces.shape[1:])
    for k in order:
        pieces = lax.all_to_all(pieces, axes[k], split_axis=k, concat_axis=k, tiled=True)
    return pieces.reshape(-1, *pieces.shape[len(axes) :])


def core_and_chips(shard, groups, order, split_dim, concat_dim):
    devices = lax.axis_size(groups[0]) * lax.axis_size(groups[1])
    pieces = split_up(shard, split_dim, devices)
    return in_order(turned_blocks(pieces, groups, order), concat_dim)


def anterp_tables(theta_count, phi_count, theta_child, phi_child):
    theta_fine = math.pi * (jnp.arange(theta_count, dtype=jnp.float32) + 0.5) / theta_count
    theta_coarse = math.pi * (jnp.arange(theta_child, dtype=jnp.float32) + 0.5) / theta_child
    orders = jnp.arange(theta_child, dtype=jnp.float32)
    weights = jnp.where(orders > 0, 2.0, 1.0).astype(jnp.float32)
    theta_matrix = (
        jnp.dot(
            jnp.cos(jnp.outer(theta_coarse, orders)) * weights,
            jnp.cos(jnp.outer(theta_fine, orders)).T,
            precision=lax.Precision.HIGHEST,
        )
        / theta_count
    )
    phi_fine = 2.0 * math.pi * jnp.arange(phi_count, dtype=jnp.float32) / phi_count
    phi_coarse = 2.0 * math.pi * jnp.arange(phi_child, dtype=jnp.float32) / phi_child
    phi_modes = jnp.arange(phi_child // 2 + 1, dtype=jnp.float32)
    mode_weights = jnp.where((phi_modes > 0) & (phi_modes < phi_child // 2), 2.0, 1.0).astype(
        jnp.float32
    )
    cos_part = jnp.dot(
        jnp.cos(jnp.outer(phi_coarse, phi_modes)) * mode_weights,
        jnp.cos(jnp.outer(phi_fine, phi_modes)).T,
        precision=lax.Precision.HIGHEST,
    )
    sin_part = jnp.dot(
        jnp.sin(jnp.outer(phi_coarse, phi_modes)) * mode_weights,
        jnp.sin(jnp.outer(phi_fine, phi_modes)).T,
        precision=lax.Precision.HIGHEST,
    )
    phi_matrix = (cos_part + sin_part) / phi_count
    sin_theta = jnp.sin(theta_fine)[:, None]
    dir_x = sin_theta * jnp.cos(phi_fine)[None, :]
    dir_y = sin_theta * jnp.sin(phi_fine)[None, :]
    dir_z = jnp.cos(theta_fine)[:, None] * jnp.ones((1, phi_count), jnp.float32)
    return (theta_matrix, phi_matrix, dir_x, dir_y, dir_z)


def anterpolate(parents, octants, child_theta, child_phi):
    tables = anterp_tables(parents.shape[2], parents.shape[3], child_theta, child_phi)
    theta_matrix, phi_matrix, dir_x, dir_y, dir_z = tables
    sign_x = (1 - 2 * (octants % 2)).astype(jnp.float32)[:, None, None]
    sign_y = (1 - 2 * (octants // 2 % 2)).astype(jnp.float32)[:, None, None]
    sign_z = (1 - 2 * (octants // 4)).astype(jnp.float32)[:, None, None]
    phase_arg = shift_reach * (sign_x * dir_x + sign_y * dir_y + sign_z * dir_z)
    cosine = jnp.cos(phase_arg)
    sine_part = jnp.sin(phase_arg)
    real_part = parents[:, 0] * cosine - parents[:, 1] * sine_part
    imag_part = parents[:, 0] * sine_part + parents[:, 1] * cosine
    shifted = jnp.stack([real_part, imag_part], axis=1)
    coarse = jnp.einsum("jt,sktf->skjf", theta_matrix, shifted, precision=lax.Precision.HIGHEST)
    return jnp.einsum("skjf,gf->skjg", coarse, phi_matrix, precision=lax.Precision.HIGHEST)


def on_device(patterns, operators, partners, operator_index, child_parent, child_octant):
    group_rows = patterns.shape[0]
    edge_band = group_rows // 4
    group_index = lax.axis_index("group")
    extended = with_halo(patterns, (("group", 0),), edge_band)
    local_partners = partners - (group_index * group_rows - edge_band)

    def add_partner(column, running):
        partner_rows = jnp.take(
            extended, lax.dynamic_index_in_dim(local_partners, column, 1, keepdims=False), axis=0
        )
        factors = jnp.take(
            operators, lax.dynamic_index_in_dim(operator_index, column, 1, keepdims=False), axis=0
        )
        real_part = factors[:, 0] * partner_rows[:, 0] - factors[:, 1] * partner_rows[:, 1]
        imag_part = factors[:, 0] * partner_rows[:, 1] + factors[:, 1] * partner_rows[:, 0]
        return running + jnp.stack([real_part, imag_part], axis=1)

    translated = lax.fori_loop(
        0, partners.shape[1], add_partner, jnp.zeros(patterns.shape, jnp.float32)
    )
    parents = core_and_chips(translated, (("member_0", "member_1"), "member_2"), (1, 0), 0, 2)
    per_member = parents.shape[0]
    member_index = lax.axis_index(MEMBER)
    member_count = lax.axis_size(MEMBER)
    local_parent = child_parent - group_index * group_rows
    capacity = 3 * per_member
    owner_member = local_parent // per_member
    onehot = (owner_member[:, None] == jnp.arange(member_count, dtype=jnp.int32)[None, :]).astype(
        jnp.int32
    )
    before = jnp.cumsum(onehot, axis=0) - onehot
    child_rank = jnp.sum(before * onehot, axis=1)
    is_mine = owner_member == member_index
    slot_pick = (
        is_mine[None, :] & (child_rank[None, :] == jnp.arange(capacity, dtype=jnp.int32)[:, None])
    ).astype(jnp.int32)
    slot_parent = jnp.sum(slot_pick * (local_parent % per_member)[None, :], axis=1)
    slot_octant = jnp.sum(slot_pick * child_octant[None, :], axis=1)
    results = anterpolate(jnp.take(parents, slot_parent, axis=0), slot_octant, NTC, NPC)
    received = lax.all_to_all(results, MEMBER, split_axis=2, concat_axis=0, tiled=True)
    take_index = owner_member * capacity + child_rank
    return jnp.take(received, take_index, axis=0)


def solution(mesh):
    finer = Mesh(
        mesh.devices.reshape(mesh.shape["group"], 4, 4, 2),
        ("group", "member_0", "member_1", "member_2"),
    )
    in_specs = (
        P("group", None, MEMBER, None),
        P(None, None, MEMBER, None),
        P("group", None),
        P("group", None),
        P("group"),
        P("group"),
    )
    out_specs = P("group", None, MEMBER, None)
    return jax.shard_map(
        on_device, mesh=finer, in_specs=in_specs, out_specs=out_specs, check_vma=False
    )
```

profile of v0, /device:TPU:1, one launch (start us, length us, event | category | flops | bytes accessed | tf_op | source)
XLA Modules:
  0.0 131.3 jit_solution(13985915814600639596)
XLA Ops:
  1.2 4.4 %collective-permute-start = (f32[8,2,8,512]{3,2,1,0:T(8,128)S(1)}, f32[8,2,8,512]{3,2,1,0:T(8,128)S(1)}, u32[]{:S(2)}, u32[]{:S(2)}) collective-permute-start(f32[8,2,8,512]{3,2,1,0:T(8,128)S(1)} %get-tuple-element.164), channel_id=1, source_target_pairs={{0,32},{32,64},{64,96},{96,128},{128,160},{160,192},{192,224},{1,3... | collective-permute-start | bytes 786440 | tf_op jit(solution)/shard_map/ppermute | solution.py:25
  5.6 1.3 collective-permute-start.1
  10.5 4.2 %collective-permute-done.1 = f32[8,2,8,512]{3,2,1,0:T(8,128)S(1)} collective-permute-done((f32[8,2,8,512]{3,2,1,0:T(8,128)S(1)}, f32[8,2,8,512]{3,2,1,0:T(8,128)S(1)}, u32[]{:S(2)}, u32[]{:S(2)}) %collective-permute-start.1) | collective-permute-done | bytes 262176 | tf_op jit(solution)/shard_map/ppermute | solution.py:27
  14.7 1.3 pad_maximum_fusion
  16.0 49.5 %while.14 = (s32[]{:T(128)}, f32[32,2,8,512]{3,2,1,0:T(8,128)S(1)}, s32[32,8]{0,1:T(8,128)}, f32[100,2,8,512]{3,2,1,0:T(8,128)}, s32[32,8]{0,1:T(8,128)S(1)}, /*...) while((s32[]{:T(128)}, f32[32,2,8,512]{3,2,1,0:T(8,128)S(1)}, s32[32,8]{0,1:T(8,128)}, ...), condition=%wide.region_3.4_spmd.clone, body=%wide.region_2.3_spmd.clone.sunk | while | flops 2099587 | bytes 14689507 | solution.py:131
  16.7 2.5 %gather_fusion.1 = f32[32,2,8,512]{3,2,1,0:T(8,128)S(1)} fusion(f32[100,2,8,512]{3,2,1,0:T(8,128)} %get-tuple-element.243, s32[1024]{0:T(1024)S(1)} %pad_clamp_fusion.6), kind=kCustom, calls=%fused_computation.clone.clone.1 | custom fusion | bytes 2097280 | tf_op jit(solution)/shard_map/while/body/eval_jaxpr/jit(_take)/gather | solution.py:124
  19.4 2.0 %gather_fusion = f32[32,2,8,512]{3,2,1,0:T(8,128)S(1)} fusion(f32[48,2,8,512]{3,2,1,0:T(8,128)} %get-tuple-element.245, s32[1024]{0:T(1024)S(1)} %pad_clamp_fusion.5), kind=kCustom, calls=%fused_computation.1.clone.clone.1 | custom fusion | bytes 2097280 | tf_op jit(solution)/shard_map/while/body/eval_jaxpr/jit(_take)/gather | solution.py:121
  22.9 2.5 %gather_fusion.1 = f32[32,2,8,512]{3,2,1,0:T(8,128)S(1)} fusion(f32[100,2,8,512]{3,2,1,0:T(8,128)} %get-tuple-element.243, s32[1024]{0:T(1024)S(1)} %pad_clamp_fusion.6), kind=kCustom, calls=%fused_computation.clone.clone.1 | custom fusion | bytes 2097280 | tf_op jit(solution)/shard_map/while/body/eval_jaxpr/jit(_take)/gather | solution.py:124
  25.6 2.0 %gather_fusion = f32[32,2,8,512]{3,2,1,0:T(8,128)S(1)} fusion(f32[48,2,8,512]{3,2,1,0:T(8,128)} %get-tuple-element.245, s32[1024]{0:T(1024)S(1)} %pad_clamp_fusion.5), kind=kCustom, calls=%fused_computation.1.clone.clone.1 | custom fusion | bytes 2097280 | tf_op jit(solution)/shard_map/while/body/eval_jaxpr/jit(_take)/gather | solution.py:121
  29.1 2.5 %gather_fusion.1 = f32[32,2,8,512]{3,2,1,0:T(8,128)S(1)} fusion(f32[100,2,8,512]{3,2,1,0:T(8,128)} %get-tuple-element.243, s32[1024]{0:T(1024)S(1)} %pad_clamp_fusion.6), kind=kCustom, calls=%fused_computation.clone.clone.1 | custom fusion | bytes 2097280 | tf_op jit(solution)/shard_map/while/body/eval_jaxpr/jit(_take)/gather | solution.py:124
  31.8 2.0 %gather_fusion = f32[32,2,8,512]{3,2,1,0:T(8,128)S(1)} fusion(f32[48,2,8,512]{3,2,1,0:T(8,128)} %get-tuple-element.245, s32[1024]{0:T(1024)S(1)} %pad_clamp_fusion.5), kind=kCustom, calls=%fused_computation.1.clone.clone.1 | custom fusion | bytes 2097280 | tf_op jit(solution)/shard_map/while/body/eval_jaxpr/jit(_take)/gather | solution.py:121
  35.3 2.5 %gather_fusion.1 = f32[32,2,8,512]{3,2,1,0:T(8,128)S(1)} fusion(f32[100,2,8,512]{3,2,1,0:T(8,128)} %get-tuple-element.243, s32[1024]{0:T(1024)S(1)} %pad_clamp_fusion.6), kind=kCustom, calls=%fused_computation.clone.clone.1 | custom fusion | bytes 2097280 | tf_op jit(solution)/shard_map/while/body/eval_jaxpr/jit(_take)/gather | solution.py:124
  38.0 2.0 %gather_fusion = f32[32,2,8,512]{3,2,1,0:T(8,128)S(1)} fusion(f32[48,2,8,512]{3,2,1,0:T(8,128)} %get-tuple-element.245, s32[1024]{0:T(1024)S(1)} %pad_clamp_fusion.5), kind=kCustom, calls=%fused_computation.1.clone.clone.1 | custom fusion | bytes 2097280 | tf_op jit(solution)/shard_map/while/body/eval_jaxpr/jit(_take)/gather | solution.py:121
  41.5 2.5 %gather_fusion.1 = f32[32,2,8,512]{3,2,1,0:T(8,128)S(1)} fusion(f32[100,2,8,512]{3,2,1,0:T(8,128)} %get-tuple-element.243, s32[1024]{0:T(1024)S(1)} %pad_clamp_fusion.6), kind=kCustom, calls=%fused_computation.clone.clone.1 | custom fusion | bytes 2097280 | tf_op jit(solution)/shard_map/while/body/eval_jaxpr/jit(_take)/gather | solution.py:124
  44.2 2.0 %gather_fusion = f32[32,2,8,512]{3,2,1,0:T(8,128)S(1)} fusion(f32[48,2,8,512]{3,2,1,0:T(8,128)} %get-tuple-element.245, s32[1024]{0:T(1024)S(1)} %pad_clamp_fusion.5), kind=kCustom, calls=%fused_computation.1.clone.clone.1 | custom fusion | bytes 2097280 | tf_op jit(solution)/shard_map/while/body/eval_jaxpr/jit(_take)/gather | solution.py:121
  47.6 2.5 %gather_fusion.1 = f32[32,2,8,512]{3,2,1,0:T(8,128)S(1)} fusion(f32[100,2,8,512]{3,2,1,0:T(8,128)} %get-tuple-element.243, s32[1024]{0:T(1024)S(1)} %pad_clamp_fusion.6), kind=kCustom, calls=%fused_computation.clone.clone.1 | custom fusion | bytes 2097280 | tf_op jit(solution)/shard_map/while/body/eval_jaxpr/jit(_take)/gather | solution.py:124
  50.4 2.0 %gather_fusion = f32[32,2,8,512]{3,2,1,0:T(8,128)S(1)} fusion(f32[48,2,8,512]{3,2,1,0:T(8,128)} %get-tuple-element.245, s32[1024]{0:T(1024)S(1)} %pad_clamp_fusion.5), kind=kCustom, calls=%fused_computation.1.clone.clone.1 | custom fusion | bytes 2097280 | tf_op jit(solution)/shard_map/while/body/eval_jaxpr/jit(_take)/gather | solution.py:121
  53.8 2.5 %gather_fusion.1 = f32[32,2,8,512]{3,2,1,0:T(8,128)S(1)} fusion(f32[100,2,8,512]{3,2,1,0:T(8,128)} %get-tuple-element.243, s32[1024]{0:T(1024)S(1)} %pad_clamp_fusion.6), kind=kCustom, calls=%fused_computation.clone.clone.1 | custom fusion | bytes 2097280 | tf_op jit(solution)/shard_map/while/body/eval_jaxpr/jit(_take)/gather | solution.py:124
  56.5 2.0 %gather_fusion = f32[32,2,8,512]{3,2,1,0:T(8,128)S(1)} fusion(f32[48,2,8,512]{3,2,1,0:T(8,128)} %get-tuple-element.245, s32[1024]{0:T(1024)S(1)} %pad_clamp_fusion.5), kind=kCustom, calls=%fused_computation.1.clone.clone.1 | custom fusion | bytes 2097280 | tf_op jit(solution)/shard_map/while/body/eval_jaxpr/jit(_take)/gather | solution.py:121
  60.0 2.5 %gather_fusion.1 = f32[32,2,8,512]{3,2,1,0:T(8,128)S(1)} fusion(f32[100,2,8,512]{3,2,1,0:T(8,128)} %get-tuple-element.243, s32[1024]{0:T(1024)S(1)} %pad_clamp_fusion.6), kind=kCustom, calls=%fused_computation.clone.clone.1 | custom fusion | bytes 2097280 | tf_op jit(solution)/shard_map/while/body/eval_jaxpr/jit(_take)/gather | solution.py:124
  62.7 2.0 %gather_fusion = f32[32,2,8,512]{3,2,1,0:T(8,128)S(1)} fusion(f32[48,2,8,512]{3,2,1,0:T(8,128)} %get-tuple-element.245, s32[1024]{0:T(1024)S(1)} %pad_clamp_fusion.5), kind=kCustom, calls=%fused_computation.1.clone.clone.1 | custom fusion | bytes 2097280 | tf_op jit(solution)/shard_map/while/body/eval_jaxpr/jit(_take)/gather | solution.py:121
  65.6 5.9 %all_to_all.28 = f32[16,2,1,2,8,512]{5,4,3,0,2,1:T(8,128)S(1)} all-to-all(f32[16,2,1,2,8,512]{5,4,3,0,2,1:T(8,128)S(1)} %copy.22), channel_id=1, replica_groups=mesh['group'=8,'member_0'=4,'member_1'=4,'member_2'=2] {'member_2'}, dimensions={1} | all-to-all | bytes 2097152 | tf_op jit(solution)/shard_map/all_to_all | solution.py:50
  72.6 6.8 %all-to-all-start.1 = ((f32[16,2,1,2,8,512]{5,4,3,1,2,0:T(8,128)}), f32[16,2,1,2,8,512]{5,4,3,1,2,0:T(8,128)S(1)}, u32[]{:S(2)}, u32[]{:S(2)}) async-start(f32[16,2,1,2,8,512]{5,4,3,1,2,0:T(8,128)} %copy.23), calls=%async_computation.1 | async-start | bytes 2097152 | tf_op jit(solution)/shard_map/all_to_all | solution.py:50
  80.3 3.3 %fusion.12 = f32[256,512]{1,0:T(8,128)S(1)} fusion(f32[512]{0:T(512)S(1)} %iota_multiply_fusion.6, f32[129]{0:T(256)S(1)} %and_select_fusion, f32[256]{0:T(256)S(1)} %iota_multiply_fusion.7), kind=kOutput, calls=%fused_computation.34 | convolution fusion | flops 203031552 | bytes 527876 | tf_op jit(solution)/shard_map/dot_general | solution.py:79
  83.6 3.3 %fusion.9 = f32[256,512,1,1]{1,0,3,2:T(8,128)S(1)} fusion(f32[256,512]{1,0:T(8,128)S(1)} %fusion.12, f32[512]{0:T(512)S(1)} %iota_multiply_fusion.6, f32[129]{0:T(256)S(1)} %and_select_fusion, f32[256]{0:T(256)S(1)} %iota_multiply_fusion.7), kind=kOutput, calls=%fused_computation.28 | convolution fusion | flops 203293696 | bytes 1052164 | tf_op jit(solution)/shard_map/dot_general | solution.py:84
  87.2 8.5 %all-to-all-done.1 = f32[16,2,1,2,8,512]{5,4,3,1,2,0:T(8,128)S(1)} async-done(((f32[16,2,1,2,8,512]{5,4,3,1,2,0:T(8,128)}), f32[16,2,1,2,8,512]{5,4,3,1,2,0:T(8,128)S(1)}, u32[]{:S(2)}, u32[]{:S(2)}) %all-to-all-start.1) | async-done | bytes 1048608 | tf_op jit(solution)/shard_map/all_to_all | solution.py:50
  96.2 6.2 %multiply_subtract_fusion.1 = (f32[3,1,256,512]{2,3,1,0:T(8,128)S(1)}, f32[3,1,256,512]{2,3,1,0:T(8,128)S(1)}) fusion(f32[256,512]{0,1:T(8,128)S(1)} %copy.26, f32[256,512]{0,1:T(8,128)S(1)} %copy.25, f32[256]{0:T(256)S(1)} %fusion.45, f32[3]{0:T(128)S(1)} %get-tuple-element.169, f32[256,512]{0,1:T(8,128)S(1)} %get-tuple-element.167, ...), kind=kLoop, calls=%fused_computation.22 | loop fusion | flops 4718592 | bytes 5243940 | tf_op jit(solution)/shard_map/sub | solution.py:106
  102.4 2.7 %fusion = f32[3,2,512,128]{3,2,1,0:T(8,128)S(1)} fusion(f32[128,256,1,1]{1,0,3,2:T(8,128)S(1)} %fusion.10, f32[3,1,256,512]{2,3,1,0:T(8,128)S(1)} %get-tuple-element.161, f32[3,1,256,512]{2,3,1,0:T(8,128)S(1)} %get-tuple-element.160), kind=kOutput, calls=%fused_computation.14 | convolution fusion | flops 1208745984 | bytes 4849664 | tf_op jit(solution)/shard_map/jt,sktf->skjf/dot_general | solution.py:109
  105.1 2.7 %fusion.4 = f32[3,2,128,256]{3,2,1,0:T(8,128)S(1)} fusion(f32[256,512,1,1]{1,0,3,2:T(8,128)S(1)} %fusion.9, f32[3,2,512,128]{3,2,1,0:T(8,128)S(1)} %fusion), kind=kOutput, calls=%fused_computation.19 | convolution fusion | flops 1207959552 | bytes 2883584 | tf_op jit(solution)/shard_map/skjf,gf->skjg/dot_general | solution.py:110
  107.8 1.5 %copy.28 = f32[3,2,128,256]{3,1,0,2:T(2,128)} copy(f32[3,2,128,256]{3,2,1,0:T(8,128)S(1)} %fusion.4) | data formatting | bytes 1572864 | tf_op jit(solution)/shard_map/skjf,gf->skjg/dot_general | solution.py:110
  109.3 5.7 %all-to-all-start.2 = ((f32[3,2,128,256]{3,1,0,2:T(2,128)}), f32[3,2,128,256]{3,1,0,2:T(2,128)S(1)}, u32[]{:S(2)}, u32[]{:S(2)}) async-start(f32[3,2,128,256]{3,1,0,2:T(2,128)} %copy.28), calls=%async_computation.2 | async-start | bytes 1572864 | tf_op jit(solution)/shard_map/all_to_all | solution.py:153
  115.0 14.3 %all-to-all-done.2 = f32[3,2,128,256]{3,1,0,2:T(2,128)S(1)} async-done(((f32[3,2,128,256]{3,1,0,2:T(2,128)}), f32[3,2,128,256]{3,1,0,2:T(2,128)S(1)}, u32[]{:S(2)}, u32[]{:S(2)}) %all-to-all-start.2) | async-done | bytes 786464 | tf_op jit(solution)/shard_map/all_to_all | solution.py:153
  (89 shorter events, 22.1 us)
Async XLA Ops:
  0.0 14.7 %copy-start = (f32[32,2,8,512]{3,2,1,0:T(8,128)S(1)}, f32[32,2,8,512]{3,2,1,0:T(8,128)}, u32[]{:S(2)}) copy-start(f32[32,2,8,512]{3,2,1,0:T(8,128)} %param.8) | copy-start | bytes 3145732
  1.2 9.3 %collective-permute-start = (f32[8,2,8,512]{3,2,1,0:T(8,128)S(1)}, f32[8,2,8,512]{3,2,1,0:T(8,128)S(1)}, u32[]{:S(2)}, u32[]{:S(2)}) collective-permute-start(f32[8,2,8,512]{3,2,1,0:T(8,128)S(1)} %get-tuple-element.164), channel_id=1, source_target_pairs={{0,32},{32,64},{64,96},{96,128},{128,160},{160,192},{192,224},{1,3... | collective-permute-start | bytes 786440 | tf_op jit(solution)/shard_map/ppermute | solution.py:25
  5.6 9.1 %collective-permute-start.1 = (f32[8,2,8,512]{3,2,1,0:T(8,128)S(1)}, f32[8,2,8,512]{3,2,1,0:T(8,128)S(1)}, u32[]{:S(2)}, u32[]{:S(2)}) collective-permute-start(f32[8,2,8,512]{3,2,1,0:T(8,128)S(1)} %get-tuple-element.165), channel_id=1, source_target_pairs={{32,0},{64,32},{96,64},{128,96},{160,128},{192,160},{224,192},{33,... | collective-permute-start | bytes 786440 | tf_op jit(solution)/shard_map/ppermute | solution.py:27
  72.6 23.1 %all-to-all-start.1 = ((f32[16,2,1,2,8,512]{5,4,3,1,2,0:T(8,128)}), f32[16,2,1,2,8,512]{5,4,3,1,2,0:T(8,128)S(1)}, u32[]{:S(2)}, u32[]{:S(2)}) async-start(f32[16,2,1,2,8,512]{5,4,3,1,2,0:T(8,128)} %copy.23), calls=%async_computation.1 | async-start | bytes 2097152 | tf_op jit(solution)/shard_map/all_to_all | solution.py:50
  109.3 20.0 %all-to-all-start.2 = ((f32[3,2,128,256]{3,1,0,2:T(2,128)}), f32[3,2,128,256]{3,1,0,2:T(2,128)S(1)}, u32[]{:S(2)}, u32[]{:S(2)}) async-start(f32[3,2,128,256]{3,1,0,2:T(2,128)} %copy.28), calls=%async_computation.2 | async-start | bytes 1572864 | tf_op jit(solution)/shard_map/all_to_all | solution.py:153
where the time goes:
time: 134 us; the launch traced here: 131 us
  local copies, waits for them, and re-layouts  41.9 us (31%)
  waiting for transfers between devices  27.9 us (21%)
  other arithmetic  23.8 us (18%)
  starting transfers between devices  18.1 us (14%)
  matrix products  12.9 us (10%)
  blocking collectives  5.88 us (4%)
    gather x8, local copies, waits for them, and re-layouts, add_partner(): jnp.take(operators, lax.dynamic_index_in_dim(operator_index, column, 1, k...  20.3 us
    gather x8, local copies, waits for them, and re-layouts, add_partner(): jnp.take(extended, lax.dynamic_index_in_dim(local_partners, column, 1, ke...  16.2 us
    all_to_all x1, waiting for transfers between devices, on_device(): lax.all_to_all(results, MEMBER, split_axis=2, concat_axis=0, tiled=True)  14.3 us
    all_to_all x1, waiting for transfers between devices, turned_blocks(): lax.all_to_all(pieces, axes[k], split_axis=k, concat_axis=k, tiled=True)  8.48 us
    all_to_all x1, starting transfers between devices, turned_blocks(): lax.all_to_all(pieces, axes[k], split_axis=k, concat_axis=k, tiled=True)  6.75 us
    sub x1, other arithmetic, anterpolate(): real_part = parents[:, 0] * cosine - parents[:, 1] * sine_part  6.18 us
    all_to_all x1, blocking collectives, turned_blocks(): lax.all_to_all(pieces, axes[k], split_axis=k, concat_axis=k, tiled=True)  5.88 us
    all_to_all x1, starting transfers between devices, on_device(): lax.all_to_all(results, MEMBER, split_axis=2, concat_axis=0, tiled=True)  5.68 us
  transfers between devices with their start and end apart: 4, of which 4 were waited for; matrix products, arithmetic and copies ran while one was open for 8% of the time, Pallas kernels for 0%

commit v1 on v0

v1 whole, which is shorter than its diff:
```python
import functools

import jax
import jax.numpy as jnp
import ml_dtypes
import numpy as np
from jax import lax
from jax.experimental import pallas as pl
from jax.experimental.pallas import tpu as pltpu
from jax.sharding import PartitionSpec as P

MESH = pl.DeviceIdType.MESH

NT, NP, NTC, NPC = 256, 512, 128, 256
NPART = 8
CL = 32
CH = 64
BAND = 8
MEM = 32
LAT = NT // MEM
OUT_LAT = NTC // MEM
PER = CH // MEM
REACH = 6.0


def split(values):
    high = values.astype(ml_dtypes.bfloat16)
    low = (values - high.astype(np.float64)).astype(ml_dtypes.bfloat16)
    return high, low


def tables():
    theta_fine = np.pi * (np.arange(NT) + 0.5) / NT
    theta_coarse = np.pi * (np.arange(NTC) + 0.5) / NTC
    orders = np.arange(NTC)
    weights = np.where(orders > 0, 2.0, 1.0)
    theta = (np.cos(np.outer(theta_coarse, orders)) * weights) @ np.cos(np.outer(theta_fine, orders)).T / NT
    phi_fine = 2.0 * np.pi * np.arange(NP) / NP
    phi_coarse = 2.0 * np.pi * np.arange(NPC) / NPC
    modes = np.arange(NPC // 2 + 1)
    mode_weights = np.where((modes > 0) & (modes < NPC // 2), 2.0, 1.0)
    phi = (
        (np.cos(np.outer(phi_coarse, modes)) * mode_weights) @ np.cos(np.outer(phi_fine, modes)).T
        + (np.sin(np.outer(phi_coarse, modes)) * mode_weights) @ np.sin(np.outer(phi_fine, modes)).T
    ) / NP
    big = np.zeros((MEM, 2, OUT_LAT, MEM, 2, LAT))
    blocks = theta.reshape(MEM, OUT_LAT, MEM, LAT)
    for part in range(2):
        big[:, part, :, :, part, :] = blocks
    theta_high, theta_low = split(big.reshape(MEM * 2 * OUT_LAT, MEM * 2 * LAT))
    phi_high, phi_low = split(phi.T)
    arg = REACH * np.sin(theta_fine)[:, None] * np.cos(phi_fine)[None, :]
    wave_x = np.stack([np.cos(arg), np.sin(arg)]).reshape(2, MEM, LAT, NP).swapaxes(0, 1)
    arg = np.broadcast_to(REACH * np.cos(theta_fine)[:, None], (NT, 128))
    wave_z = np.stack([np.cos(arg), np.sin(arg)]).reshape(2, MEM, LAT, 128).swapaxes(0, 1)
    return (
        wave_x.astype(np.float32),
        wave_z.astype(np.float32),
        phi_high,
        phi_low,
        theta_high,
        theta_low,
    )


def times(a, b):
    return a[0] * b[0] - a[1] * b[1], a[0] * b[1] + a[1] * b[0]


def halves(x):
    high = x.astype(jnp.bfloat16)
    return high, (x - high.astype(jnp.float32)).astype(jnp.bfloat16)


def dot(a, b):
    return jnp.dot(a, b, preferred_element_type=jnp.float32)


def kernel(
    index,
    patterns, operators, wave_x_in, wave_z_in, phi_high_in, phi_low_in, theta_high_in, theta_low_in,
    out,
    own, wide, ops, wave_x, wave_z, phi_high, phi_low, theta_high, theta_low,
    phase, translated, high, low, made, got, thin,
    load_sem, halo_send, halo_recv, send_sem, recv_sem, back_send, back_recv,
):
    group = lax.axis_index("group")
    me = lax.axis_index("member")
    groups = lax.axis_size("group")
    above = lax.rem(group + 1, groups)
    below = lax.rem(group + groups - 1, groups)

    def load(k, src, dst):
        return pltpu.make_async_copy(src, dst, load_sem.at[k])

    loads = [
        load(0, patterns, own),
        load(1, operators, ops),
        load(2, wave_x_in.at[me], wave_x),
        load(3, wave_z_in.at[me], wave_z),
        load(4, patterns, wide.at[pl.ds(BAND, CL)]),
        load(5, phi_high_in, phi_high),
        load(6, phi_low_in, phi_low),
        load(7, theta_high_in, theta_high),
        load(8, theta_low_in, theta_low),
    ]
    for one in loads:
        one.start()

    def other(r):
        y = lax.rem(me // 8 + r // 8, 4)
        x = lax.rem(lax.rem(me // 2, 4) + lax.rem(r // 2, 4), 4)
        c = lax.rem(me + r, 2)
        return y * 8 + x * 2 + c

    barrier = pltpu.get_barrier_semaphore()
    pl.semaphore_signal(barrier, inc=1, device_id=(above, me), device_id_type=MESH)
    pl.semaphore_signal(barrier, inc=1, device_id=(below, me), device_id_type=MESH)

    @pl.loop(1, MEM)
    def _(r):
        pl.semaphore_signal(barrier, inc=1, device_id=(group, other(r)), device_id_type=MESH)

    pl.semaphore_wait(barrier, MEM + 1)

    up = pltpu.make_async_remote_copy(
        src_ref=patterns.at[pl.ds(CL - BAND, BAND)],
        dst_ref=wide.at[pl.ds(0, BAND)],
        send_sem=halo_send.at[0],
        recv_sem=halo_recv.at[0],
        device_id=(above, me),
        device_id_type=MESH,
    )
    down = pltpu.make_async_remote_copy(
        src_ref=patterns.at[pl.ds(0, BAND)],
        dst_ref=wide.at[pl.ds(CL + BAND, BAND)],
        send_sem=halo_send.at[1],
        recv_sem=halo_recv.at[1],
        device_id=(below, me),
        device_id_type=MESH,
    )
    up.start()
    down.start()

    loads[2].wait()
    loads[3].wait()
    x_real, x_imag = wave_x[0], wave_x[1]

    def turned(v):
        return jnp.concatenate([v[:, NP - NP // 4 :], v[:, : NP - NP // 4]], axis=1)

    y_real, y_imag = turned(x_real), turned(x_imag)
    z_real = jnp.concatenate([wave_z[0]] * (NP // 128), axis=1)
    z_imag = jnp.concatenate([wave_z[1]] * (NP // 128), axis=1)
    for octant in range(8):
        sx, sy, sz = 1 - 2 * (octant % 2), 1 - 2 * (octant // 2 % 2), 1 - 2 * (octant // 4)
        xy = times((x_real, sx * x_imag), (y_real, sy * y_imag))
        full = times(xy, (z_real, sz * z_imag))
        phase[octant, 0], phase[octant, 1] = full

    def translate(cluster, cells):
        real = jnp.zeros((LAT, NP), jnp.float32)
        imag = jnp.zeros((LAT, NP), jnp.float32)
        for p in range(NPART):
            cell = cells[index[cluster, p]]
            factor = ops[index[cluster, NPART + p]]
            part = times(factor, cell)
            real, imag = real + part[0], imag + part[1]
        translated[cluster, 0] = real
        translated[cluster, 1] = imag

    loads[0].wait()
    loads[1].wait()

    @pl.loop(BAND, CL - BAND)
    def _(cluster):
        translate(cluster, own)

    for one in loads[4:]:
        one.wait()
    up.wait()
    down.wait()

    @pl.loop(0, 2 * BAND)
    def _(n):
        translate(jnp.where(n < BAND, n, n + CL - 2 * BAND), wide)

    def out_copy(r):
        return pltpu.make_async_remote_copy(
            src_ref=made.at[r],
            dst_ref=got.at[me],
            send_sem=send_sem.at[r],
            recv_sem=recv_sem.at[r],
            device_id=(group, other(r)),
            device_id_type=MESH,
        )

    def shift_and_reduce(first, count):
        @pl.loop(0, count)
        def _(i):
            member = other(lax.rem(first + i, MEM))
            for k in range(PER):
                parent = translated[index[member, 2 * NPART + k]]
                moved = times(parent, phase[index[member, 2 * NPART + PER + k]])
                both = jnp.concatenate(moved, axis=0)
                h, l = halves(both)
                rows = pl.ds(pl.multiple_of((i * PER + k) * 2 * LAT, 2 * LAT), 2 * LAT)
                high[rows, :] = h
                low[rows, :] = l

        total = count * PER * 2 * LAT
        h, l = high[:total, :], low[:total, :]
        result = dot(h, phi_high[...]) + dot(h, phi_low[...]) + dot(l, phi_high[...])
        return result.reshape(count, PER, 2, LAT, NPC)

    part = 8
    for first in range(1, MEM, part):
        block = shift_and_reduce(first, part)
        left = min(part, MEM - first)
        made[first : first + left] = block[:left]
        if left < part:
            got[me] = block[left]

        @pl.loop(first, first + left)
        def _(r):
            out_copy(r).start()

    @pl.loop(1, MEM)
    def _(r):
        out_copy(r).wait()

    for k in range(PER):
        h, l = halves(got[:, k].reshape(MEM * 2 * LAT, NPC))
        result = dot(theta_high[...], h) + dot(theta_low[...], h) + dot(theta_high[...], l)
        thin[:, k] = result.reshape(MEM, 2 * OUT_LAT, NPC)

    def back_copy(r):
        return pltpu.make_async_remote_copy(
            src_ref=thin.at[other(r)],
            dst_ref=out.at[pl.ds(me * PER, PER)],
            send_sem=back_send.at[r],
            recv_sem=back_recv.at[r],
            device_id=(group, other(r)),
            device_id_type=MESH,
        )

    @pl.loop(1, MEM)
    def _(r):
        back_copy(r).start()

    out[pl.ds(me * PER, PER)] = thin[me]

    @pl.loop(1, MEM)
    def _(r):
        back_copy(r).wait()


def on_device(patterns, operators, partners, operator_index, child_parent, child_octant, *, constants):
    f32, bf16 = jnp.float32, jnp.bfloat16
    smem = pl.BlockSpec(memory_space=pltpu.SMEM)
    hbm = pl.BlockSpec(memory_space=pltpu.HBM)
    dma = pltpu.SemaphoreType.DMA
    start = lax.axis_index("group") * CL
    cluster = jnp.arange(CL)[:, None]
    inner = (cluster >= BAND) & (cluster < CL - BAND)
    index = jnp.concatenate(
        [
            partners - start + jnp.where(inner, 0, BAND),
            operator_index,
            child_parent.reshape(MEM, PER) - start,
            child_octant.reshape(MEM, PER),
        ],
        axis=1,
    )
    result = pl.pallas_call(
        kernel,
        out_shape=jax.ShapeDtypeStruct((CH, 2 * OUT_LAT, NPC), f32),
        in_specs=[smem] + [hbm] * (2 + len(constants)),
        out_specs=pl.BlockSpec(memory_space=pltpu.VMEM),
        scratch_shapes=[
            pltpu.VMEM((CL, 2, LAT, NP), f32),
            pltpu.VMEM((CL + 2 * BAND, 2, LAT, NP), f32),
            pltpu.VMEM(operators.shape, f32),
            pltpu.VMEM((2, LAT, NP), f32),
            pltpu.VMEM((2, LAT, 128), f32),
            pltpu.VMEM((NP, NPC), bf16),
            pltpu.VMEM((NP, NPC), bf16),
            pltpu.VMEM((2 * NTC, 2 * NT), bf16),
            pltpu.VMEM((2 * NTC, 2 * NT), bf16),
            pltpu.VMEM((8, 2, LAT, NP), f32),
            pltpu.VMEM((CL, 2, LAT, NP), f32),
            pltpu.VMEM((256, NP), bf16),
            pltpu.VMEM((256, NP), bf16),
            pltpu.VMEM((MEM, PER, 2, LAT, NPC), f32),
            pltpu.VMEM((MEM, PER, 2, LAT, NPC), f32),
            pltpu.VMEM((MEM, PER, 2 * OUT_LAT, NPC), f32),
            dma((9,)),
            dma((2,)),
            dma((2,)),
            dma((MEM,)),
            dma((MEM,)),
            dma((MEM,)),
            dma((MEM,)),
        ],
        compiler_params=pltpu.CompilerParams(
            collective_id=0, has_side_effects=True, vmem_limit_bytes=40 * 2**20
        ),
        cost_estimate=pl.CostEstimate(flops=10**9, bytes_accessed=6 * 2**20, transcendentals=0),
    )(index, patterns, operators, *constants)
    return result.reshape(CH, 2, OUT_LAT, NPC)


def solution(mesh):
    constants = tables()
    whole = P("group", None, "member", None)
    return jax.shard_map(
        functools.partial(on_device, constants=constants),
        mesh=mesh,
        in_specs=(whole, P(None, None, "member", None), P("group", None), P("group", None), P("group"), P("group")),
        out_specs=whole,
        check_vma=False,
    )
```

time: 134 us -> 63 us (0.47); the launches traced: 131 us -> 62.5 us
  Pallas kernels: 0 us -> 49.2 us
  local copies, waits for them, and re-layouts: 41.9 us -> 12.4 us
  waiting for transfers between devices: 27.9 us -> 0 us
  other arithmetic: 23.8 us -> 0.82 us
  starting transfers between devices: 18.1 us -> 0 us
  matrix products: 12.9 us -> 0 us
  blocking collectives: 5.88 us -> 0 us
    pallas_call x0 -> x1, Pallas kernels: none -> 49.2 us  [on_device(): pl.pallas_call(kernel, out_shape=jax.ShapeDtypeStruct((CH, 2 * OUT_LAT, N...]
    gather x17 -> x0, local copies, waits for them, and re-layouts: 37.4 us -> none  [the longest x8 20.3 us: add_partner(): jnp.take(operators, lax.dynamic_index_in_dim(operator_index, column, 1, k...]
    all_to_all x2 -> x0, waiting for transfers between devices: 22.8 us -> none  [the longest x1 14.3 us: on_device(): lax.all_to_all(results, MEMBER, split_axis=2, concat_axis=0, tiled=True)]
    dot_general x5 -> x0, matrix products: 12.9 us -> none  [the longest x1 3.34 us: anterp_tables(): jnp.dot(jnp.sin(jnp.outer(phi_coarse, phi_modes)) * mode_weights, jnp.sin...]
    all_to_all x2 -> x0, starting transfers between devices: 12.4 us -> none  [the longest x1 6.75 us: turned_blocks(): lax.all_to_all(pieces, axes[k], split_axis=k, concat_axis=k, tiled=True)]
    unnamed x2 -> x18, local copies, waits for them, and re-layouts: 0.01 us -> 10.7 us
    sub x10 -> x1, other arithmetic: 8.68 us -> 0.66 us  [on_device(): child_parent.reshape(MEM, PER) - start]
    all_to_all x1 -> x0, blocking collectives: 5.88 us -> none  [turned_blocks(): lax.all_to_all(pieces, axes[k], split_axis=k, concat_axis=k, tiled=True)]
  transfers between devices with their start and end apart: 4 -> 0, of which waited for: 4 -> 0; matrix products, arithmetic and copies ran while one was open for 8% -> 0% of each run, Pallas kernels for 0% -> 0%
where the time goes in v1:
time: 63 us; the launch traced here: 62.5 us
  Pallas kernels  49.2 us (78%)
  local copies, waits for them, and re-layouts  12.4 us (20%)
  other arithmetic  0.82 us (1%)
    pallas_call x1, Pallas kernels, on_device(): pl.pallas_call(kernel, out_shape=jax.ShapeDtypeStruct((CH, 2 * OUT_LAT, N...  49.2 us
    unnamed x18, local copies, waits for them, and re-layouts  10.7 us

profile of v1, /device:TPU:1, one launch (start us, length us, event | category | flops | bytes accessed | tf_op | source)
XLA Modules:
  0.0 62.5 jit_solution(9807687578829727632)
XLA Ops:
  0.0 0.7 %broadcast_subtract_fusion = s32[64]{0:T(128)S(1)} fusion(s32[64]{0:T(128)} %param.16, s32[]{:T(128)S(6)} %mul.3), kind=kLoop, calls=%fused_computation.3 | loop fusion | flops 64 | bytes 516 | tf_op jit(solution)/shard_map/sub | solution.py:270
  0.7 0.1 sub.19
  0.8 0.8 %copy.17 = s32[32,8]{1,0:T(8,128)S(1)} copy(s32[32,8]{0,1:T(8,128)} %param.14) | data formatting | bytes 2048 | tf_op args[2]
  1.5 0.1 subtract_add_fusion
  1.6 0.8 %copy.19 = s32[32,8]{1,0:T(8,128)S(1)} copy(s32[32,8]{0,1:T(8,128)} %param.15) | data formatting | bytes 2048 | tf_op args[3]
  2.4 0.7 %reshape.22 = s32[32,2]{1,0:T(8,128)S(1)} reshape(s32[64]{0:T(128)} %param.17) | data formatting | bytes 512 | tf_op jit(solution)/shard_map/reshape | solution.py:271
  3.1 0.1 pad_add_fusion.index
  3.2 0.0 copy-start
  3.2 1.9 %copy-done = f32[100,2,8,512]{3,2,1,0:T(8,128)S(1)} copy-done((f32[100,2,8,512]{3,2,1,0:T(8,128)S(1)}, f32[100,2,8,512]{3,2,1,0:T(8,128)}, u32[]{:S(2)}) %copy-start) | copy-done | bytes 3276824
  5.1 0.0 copy-start.1
  5.1 1.2 %copy-done.1 = f32[32,2,8,512]{3,2,1,0:T(8,128)S(1)} copy-done((f32[32,2,8,512]{3,2,1,0:T(8,128)S(1)}, f32[32,2,8,512]{3,2,1,0:T(8,128)}, u32[]{:S(2)}) %copy-start.1) | copy-done | bytes 1048600
  6.4 0.0 copy-start.2
  6.4 1.2 %copy-done.2 = f32[32,2,8,512]{3,2,1,0:T(8,128)S(1)} copy-done((f32[32,2,8,512]{3,2,1,0:T(8,128)S(1)}, f32[32,2,8,512]{3,2,1,0:T(8,128)}, u32[]{:S(2)}) %copy-start.2) | copy-done | bytes 1048600
  7.6 0.0 copy-start.3
  7.6 0.9 %copy-done.3 = bf16[256,512]{1,0:T(8,128)(2,1)S(1)} copy-done((bf16[256,512]{1,0:T(8,128)(2,1)S(1)}, bf16[256,512]{1,0:T(8,128)(2,1)}, u32[]{:S(2)}) %copy-start.3) | copy-done | bytes 262168
  8.5 0.0 copy-start.4
  8.5 0.9 %copy-done.4 = bf16[256,512]{1,0:T(8,128)(2,1)S(1)} copy-done((bf16[256,512]{1,0:T(8,128)(2,1)S(1)}, bf16[256,512]{1,0:T(8,128)(2,1)}, u32[]{:S(2)}) %copy-start.4) | copy-done | bytes 262168
  9.5 0.0 copy-start.5
  9.5 0.9 %copy-done.5 = bf16[512,256]{1,0:T(8,128)(2,1)S(1)} copy-done((bf16[512,256]{1,0:T(8,128)(2,1)S(1)}, bf16[512,256]{1,0:T(8,128)(2,1)}, u32[]{:S(2)}) %copy-start.5) | copy-done | bytes 262168
  10.4 0.0 copy-start.6
  10.4 0.9 %copy-done.6 = bf16[512,256]{1,0:T(8,128)(2,1)S(1)} copy-done((bf16[512,256]{1,0:T(8,128)(2,1)S(1)}, bf16[512,256]{1,0:T(8,128)(2,1)}, u32[]{:S(2)}) %copy-start.6) | copy-done | bytes 262168
  11.4 0.0 copy-start.7
  11.4 0.9 %copy-done.7 = f32[32,2,8,128]{3,2,1,0:T(8,128)S(1)} copy-done((f32[32,2,8,128]{3,2,1,0:T(8,128)S(1)}, f32[32,2,8,128]{3,2,1,0:T(8,128)}, u32[]{:S(2)}) %copy-start.7) | copy-done | bytes 262168
  12.3 49.2 %shard_map.118 = f32[64,8,256]{2,1,0:T(8,128)S(1)} custom-call(s32[32,20]{1,0:T(8,128)S(1)} %pad_add_fusion.index, f32[32,2,8,512]{3,2,1,0:T(8,128)S(1)} %copy-done.1, f32[100,2,8,512]{3,2,1,0:T(8,128)S(1)} %copy-done, f32[32,2,8,512]{3,2,1,0:T(8,128)S(1)} %copy-done.2, f32[32,2,8,128]{3,2,1,0:T(8,128)S(1)} %copy-done.7, bf16[512,256]{1,0:T(8,128)(2,1)S(1)} %copy-done.6, ...), custom_call_target="tpu_custom_call" | custom-call | flops 1000000000 | bytes 6291456 | tf_op jit(solution)/shard_map/pallas_call | solution.py:275
  61.6 0.9 %reshape.23 = f32[64,2,4,256]{3,2,1,0:T(4,128)} reshape(f32[64,8,256]{2,1,0:T(8,128)S(1)} %shard_map.118) | data formatting | bytes 1048576 | tf_op jit(solution)/shard_map/reshape | solution.py:310
  (1 shorter events, 0.0 us)
Async XLA Ops:
  3.2 1.9 %copy-start = (f32[100,2,8,512]{3,2,1,0:T(8,128)S(1)}, f32[100,2,8,512]{3,2,1,0:T(8,128)}, u32[]{:S(2)}) copy-start(f32[100,2,8,512]{3,2,1,0:T(8,128)} %operators.1) | copy-start | bytes 9830404
  5.1 1.2 %copy-start.1 = (f32[32,2,8,512]{3,2,1,0:T(8,128)S(1)}, f32[32,2,8,512]{3,2,1,0:T(8,128)}, u32[]{:S(2)}) copy-start(f32[32,2,8,512]{3,2,1,0:T(8,128)} %patterns.1) | copy-start | bytes 3145732
  6.4 1.2 %copy-start.2 = (f32[32,2,8,512]{3,2,1,0:T(8,128)S(1)}, f32[32,2,8,512]{3,2,1,0:T(8,128)}, u32[]{:S(2)}) copy-start(f32[32,2,8,512]{3,2,1,0:T(8,128)} %constant.27.clone.wave_x_in) | copy-start | bytes 3145732
  7.6 0.9 %copy-start.3 = (bf16[256,512]{1,0:T(8,128)(2,1)S(1)}, bf16[256,512]{1,0:T(8,128)(2,1)}, u32[]{:S(2)}) copy-start(bf16[256,512]{1,0:T(8,128)(2,1)} %constant.32.clone.theta_low_in) | copy-start | bytes 786436
  8.5 0.9 %copy-start.4 = (bf16[256,512]{1,0:T(8,128)(2,1)S(1)}, bf16[256,512]{1,0:T(8,128)(2,1)}, u32[]{:S(2)}) copy-start(bf16[256,512]{1,0:T(8,128)(2,1)} %constant.31.clone.theta_high_in) | copy-start | bytes 786436
  9.5 0.9 %copy-start.5 = (bf16[512,256]{1,0:T(8,128)(2,1)S(1)}, bf16[512,256]{1,0:T(8,128)(2,1)}, u32[]{:S(2)}) copy-start(bf16[512,256]{1,0:T(8,128)(2,1)} %constant.30.clone.phi_low_in) | copy-start | bytes 786436
  10.4 0.9 %copy-start.6 = (bf16[512,256]{1,0:T(8,128)(2,1)S(1)}, bf16[512,256]{1,0:T(8,128)(2,1)}, u32[]{:S(2)}) copy-start(bf16[512,256]{1,0:T(8,128)(2,1)} %constant.29.clone.phi_high_in) | copy-start | bytes 786436
  11.4 0.9 %copy-start.7 = (f32[32,2,8,128]{3,2,1,0:T(8,128)S(1)}, f32[32,2,8,128]{3,2,1,0:T(8,128)}, u32[]{:S(2)}) copy-start(f32[32,2,8,128]{3,2,1,0:T(8,128)} %constant.28.clone.wave_z_in) | copy-start | bytes 786436

commit v2 on v1

--- a/solution.py
+++ b/solution.py
@@ -77,9 +77,9 @@
 
 
 def kernel(
-    index,
-    patterns, operators, wave_x_in, wave_z_in, phi_high_in, phi_low_in, theta_high_in, theta_low_in,
+    partners_in, factors_in, parents_in, octants_in, patterns, operators, wave_x_in, wave_z_in, phi_high_in, phi_low_in, theta_high_in, theta_low_in,
     out,
+    partners, factors, parents, octants,
     own, wide, ops, wave_x, wave_z, phi_high, phi_low, theta_high, theta_low,
     phase, translated, high, low, made, got, thin,
     load_sem, halo_send, halo_recv, send_sem, recv_sem, back_send, back_recv,
@@ -94,15 +94,19 @@
         return pltpu.make_async_copy(src, dst, load_sem.at[k])
 
     loads = [
-        load(0, patterns, own),
-        load(1, operators, ops),
-        load(2, wave_x_in.at[me], wave_x),
-        load(3, wave_z_in.at[me], wave_z),
-        load(4, patterns, wide.at[pl.ds(BAND, CL)]),
-        load(5, phi_high_in, phi_high),
-        load(6, phi_low_in, phi_low),
-        load(7, theta_high_in, theta_high),
-        load(8, theta_low_in, theta_low),
+        load(0, wave_x_in.at[me], wave_x),
+        load(1, wave_z_in.at[me], wave_z),
+        load(2, partners_in, partners),
+        load(3, factors_in, factors),
+        load(4, patterns, own),
+        load(5, operators, ops),
+        load(6, patterns, wide.at[pl.ds(BAND, CL)]),
+        load(7, parents_in, parents),
+        load(8, octants_in, octants),
+        load(9, phi_high_in, phi_high),
+        load(10, phi_low_in, phi_low),
+        load(11, theta_high_in, theta_high),
+        load(12, theta_low_in, theta_low),
     ]
     for one in loads:
         one.start()
@@ -142,8 +146,8 @@
     up.start()
     down.start()
 
-    loads[2].wait()
-    loads[3].wait()
+    for one in loads[:2]:
+        one.wait()
     x_real, x_imag = wave_x[0], wave_x[1]
 
     def turned(v):
@@ -158,32 +162,32 @@
         full = times(xy, (z_real, sz * z_imag))
         phase[octant, 0], phase[octant, 1] = full
 
-    def translate(cluster, cells):
+    def translate(cluster, cells, first):
         real = jnp.zeros((LAT, NP), jnp.float32)
         imag = jnp.zeros((LAT, NP), jnp.float32)
         for p in range(NPART):
-            cell = cells[index[cluster, p]]
-            factor = ops[index[cluster, NPART + p]]
+            cell = cells[jnp.clip(partners[p, cluster] - first, 0, cells.shape[0] - 1)]
+            factor = ops[factors[p, cluster]]
             part = times(factor, cell)
             real, imag = real + part[0], imag + part[1]
         translated[cluster, 0] = real
         translated[cluster, 1] = imag
 
-    loads[0].wait()
-    loads[1].wait()
+    for one in loads[2:6]:
+        one.wait()
 
     @pl.loop(BAND, CL - BAND)
     def _(cluster):
-        translate(cluster, own)
-
-    for one in loads[4:]:
+        translate(cluster, own, group * CL)
+
+    for one in loads[6:]:
         one.wait()
     up.wait()
     down.wait()
 
     @pl.loop(0, 2 * BAND)
     def _(n):
-        translate(jnp.where(n < BAND, n, n + CL - 2 * BAND), wide)
+        translate(jnp.where(n < BAND, n, n + CL - 2 * BAND), wide, group * CL - BAND)
 
     def out_copy(r):
         return pltpu.make_async_remote_copy(
@@ -200,8 +204,9 @@
         def _(i):
             member = other(lax.rem(first + i, MEM))
             for k in range(PER):
-                parent = translated[index[member, 2 * NPART + k]]
-                moved = times(parent, phase[index[member, 2 * NPART + PER + k]])
+                child = member * PER + k
+                parent = translated[lax.rem(parents[child], CL)]
+                moved = times(parent, phase[octants[child]])
                 both = jnp.concatenate(moved, axis=0)
                 h, l = halves(both)
                 rows = pl.ds(pl.multiple_of((i * PER + k) * 2 * LAT, 2 * LAT), 2 * LAT)
@@ -257,27 +262,18 @@
 
 def on_device(patterns, operators, partners, operator_index, child_parent, child_octant, *, constants):
     f32, bf16 = jnp.float32, jnp.bfloat16
-    smem = pl.BlockSpec(memory_space=pltpu.SMEM)
     hbm = pl.BlockSpec(memory_space=pltpu.HBM)
     dma = pltpu.SemaphoreType.DMA
-    start = lax.axis_index("group") * CL
-    cluster = jnp.arange(CL)[:, None]
-    inner = (cluster >= BAND) & (cluster < CL - BAND)
-    index = jnp.concatenate(
-        [
-            partners - start + jnp.where(inner, 0, BAND),
-            operator_index,
-            child_parent.reshape(MEM, PER) - start,
-            child_octant.reshape(MEM, PER),
-        ],
-        axis=1,
-    )
     result = pl.pallas_call(
         kernel,
         out_shape=jax.ShapeDtypeStruct((CH, 2 * OUT_LAT, NPC), f32),
-        in_specs=[smem] + [hbm] * (2 + len(constants)),
+        in_specs=[hbm] * (6 + len(constants)),
         out_specs=pl.BlockSpec(memory_space=pltpu.VMEM),
         scratch_shapes=[
+            pltpu.SMEM((NPART, CL), jnp.int32),
+            pltpu.SMEM((NPART, CL), jnp.int32),
+            pltpu.SMEM((CH,), jnp.int32),
+            pltpu.SMEM((CH,), jnp.int32),
             pltpu.VMEM((CL, 2, LAT, NP), f32),
             pltpu.VMEM((CL + 2 * BAND, 2, LAT, NP), f32),
             pltpu.VMEM(operators.shape, f32),
@@ -294,7 +290,7 @@
             pltpu.VMEM((MEM, PER, 2, LAT, NPC), f32),
             pltpu.VMEM((MEM, PER, 2, LAT, NPC), f32),
             pltpu.VMEM((MEM, PER, 2 * OUT_LAT, NPC), f32),
-            dma((9,)),
+            dma((13,)),
             dma((2,)),
             dma((2,)),
             dma((MEM,)),
@@ -303,10 +299,10 @@
             dma((MEM,)),
         ],
         compiler_params=pltpu.CompilerParams(
-            collective_id=0, has_side_effects=True, vmem_limit_bytes=40 * 2**20
+            collective_id=0, has_side_effects=True, vmem_limit_bytes=60 * 2**20
         ),
         cost_estimate=pl.CostEstimate(flops=10**9, bytes_accessed=6 * 2**20, transcendentals=0),
-    )(index, patterns, operators, *constants)
+    )(partners.T, operator_index.T, child_parent, child_octant, patterns, operators, *constants)
     return result.reshape(CH, 2, OUT_LAT, NPC)
 
 

time: 63 us -> 50.8 us (0.81)
  local copies, waits for them, and re-layouts: 12.4 us -> 1.98 us
  other arithmetic: 0.82 us -> 0 us
    unnamed x18 -> x0, local copies, waits for them, and re-layouts: 10.7 us -> none
    reshape x1, local copies, waits for them, and re-layouts: 0.94 us -> 1.98 us  [on_device(): return result.reshape(CH, 2, OUT_LAT, NPC)]
    reshape x1 -> x0, local copies, waits for them, and re-layouts: 0.75 us -> none  [on_device(): child_octant.reshape(MEM, PER)]
    sub x1 -> x0, other arithmetic: 0.66 us -> none  [on_device(): child_parent.reshape(MEM, PER) - start]
where the time goes in v2:
time: 50.8 us; the launch traced here: 50.7 us
  Pallas kernels  48.7 us (96%)
  local copies, waits for them, and re-layouts  1.98 us (4%)
    pallas_call x1, Pallas kernels, on_device(): pl.pallas_call(kernel, out_shape=jax.ShapeDtypeStruct((CH, 2 * OUT_LAT, N...  48.7 us
    reshape x1, local copies, waits for them, and re-layouts, on_device(): return result.reshape(CH, 2, OUT_LAT, NPC)  1.98 us

profile of v2, /device:TPU:1, one launch (start us, length us, event | category | flops | bytes accessed | tf_op | source)
XLA Modules:
  0.0 50.7 jit_solution(13619673824897212936)
XLA Ops:
  0.0 48.7 %shard_map.118 = f32[64,8,256]{2,1,0:T(8,128)} custom-call(s32[8,32]{1,0:T(8,128)} %bitcast.2, s32[8,32]{1,0:T(8,128)} %bitcast.3, s32[64]{0:T(128)} %parents_in.1, s32[64]{0:T(128)} %octants_in.1, f32[32,2,8,512]{3,2,1,0:T(8,128)} %patterns.1, f32[100,2,8,512]{3,2,1,0:T(8,128)} %operators.1, f32[32,2,8,512]{3,2,1,0:T(8,128)} %constant.12.clone.wave_x_in, ...), custom_call_target="tpu_custom_call" | custom-call | flops 1000000000 | bytes 6291456 | tf_op jit(solution)/shard_map/pallas_call | solution.py:267
  48.7 2.0 %reshape.3 = f32[64,2,4,256]{3,2,1,0:T(4,128)} reshape(f32[64,8,256]{2,1,0:T(8,128)} %shard_map.118) | data formatting | bytes 1048576 | tf_op jit(solution)/shard_map/reshape | solution.py:306

commit v3 on v2

--- a/solution.py
+++ b/solution.py
@@ -21,6 +21,7 @@
 OUT_LAT = NTC // MEM
 PER = CH // MEM
 REACH = 6.0
+HALO_PARTS = 1
 
 
 def split(values):
@@ -87,8 +88,8 @@
     group = lax.axis_index("group")
     me = lax.axis_index("member")
     groups = lax.axis_size("group")
-    above = lax.rem(group + 1, groups)
-    below = lax.rem(group + groups - 1, groups)
+    below, above = group - 1, group + 1
+    has_below, has_above = group > 0, group < groups - 1
 
     def load(k, src, dst):
         return pltpu.make_async_copy(src, dst, load_sem.at[k])
@@ -118,33 +119,18 @@
         return y * 8 + x * 2 + c
 
     barrier = pltpu.get_barrier_semaphore()
-    pl.semaphore_signal(barrier, inc=1, device_id=(above, me), device_id_type=MESH)
-    pl.semaphore_signal(barrier, inc=1, device_id=(below, me), device_id_type=MESH)
+
+    @pl.when(has_above)
+    def _():
+        pl.semaphore_signal(barrier, inc=1, device_id=(above, me), device_id_type=MESH)
+
+    @pl.when(has_below)
+    def _():
+        pl.semaphore_signal(barrier, inc=1, device_id=(below, me), device_id_type=MESH)
 
     @pl.loop(1, MEM)
     def _(r):
         pl.semaphore_signal(barrier, inc=1, device_id=(group, other(r)), device_id_type=MESH)
-
-    pl.semaphore_wait(barrier, MEM + 1)
-
-    up = pltpu.make_async_remote_copy(
-        src_ref=patterns.at[pl.ds(CL - BAND, BAND)],
-        dst_ref=wide.at[pl.ds(0, BAND)],
-        send_sem=halo_send.at[0],
-        recv_sem=halo_recv.at[0],
-        device_id=(above, me),
-        device_id_type=MESH,
-    )
-    down = pltpu.make_async_remote_copy(
-        src_ref=patterns.at[pl.ds(0, BAND)],
-        dst_ref=wide.at[pl.ds(CL + BAND, BAND)],
-        send_sem=halo_send.at[1],
-        recv_sem=halo_recv.at[1],
-        device_id=(below, me),
-        device_id_type=MESH,
-    )
-    up.start()
-    down.start()
 
     for one in loads[:2]:
         one.wait()
@@ -180,10 +166,53 @@
     def _(cluster):
         translate(cluster, own, group * CL)
 
+    pl.semaphore_wait(barrier, MEM - 1 + jnp.minimum(group, 1) + jnp.minimum(groups - 1 - group, 1))
+
+    width = BAND // HALO_PARTS
+
+    def up(n, to):
+        return pltpu.make_async_remote_copy(
+            src_ref=patterns.at[pl.ds(CL - BAND + n * width, width)],
+            dst_ref=wide.at[pl.ds(n * width, width)],
+            send_sem=halo_send.at[0, n],
+            recv_sem=halo_recv.at[0, n],
+            device_id=(to, me),
+            device_id_type=MESH,
+        )
+
+    def down(n, to):
+        return pltpu.make_async_remote_copy(
+            src_ref=patterns.at[pl.ds(n * width, width)],
+            dst_ref=wide.at[pl.ds(CL + BAND + n * width, width)],
+            send_sem=halo_send.at[1, n],
+            recv_sem=halo_recv.at[1, n],
+            device_id=(to, me),
+            device_id_type=MESH,
+        )
+
+    for n in range(HALO_PARTS):
+
+        @pl.when(has_above)
+        def _():
+            up(n, above).start()
+
+        @pl.when(has_below)
+        def _():
+            down(n, below).start()
+
     for one in loads[6:]:
         one.wait()
-    up.wait()
-    down.wait()
+    for n in range(HALO_PARTS):
+
+        @pl.when(has_above)
+        def _():
+            up(n, above).wait_send()
+            down(n, above).wait_recv()
+
+        @pl.when(has_below)
+        def _():
+            down(n, below).wait_send()
+            up(n, below).wait_recv()
 
     @pl.loop(0, 2 * BAND)
     def _(n):
@@ -291,8 +320,8 @@
             pltpu.VMEM((MEM, PER, 2, LAT, NPC), f32),
             pltpu.VMEM((MEM, PER, 2 * OUT_LAT, NPC), f32),
             dma((13,)),
-            dma((2,)),
-            dma((2,)),
+            dma((2, HALO_PARTS)),
+            dma((2, HALO_PARTS)),
             dma((MEM,)),
             dma((MEM,)),
             dma((MEM,)),

time: 50.8 us -> 47.1 us (0.927)
  Pallas kernels: 48.7 us -> 44.6 us
    pallas_call x1, Pallas kernels: 48.7 us -> 44.6 us  [on_device(): pl.pallas_call(kernel, out_shape=jax.ShapeDtypeStruct((CH, 2 * OUT_LAT, N...]
where the time goes in v3:
time: 47.1 us; the launch traced here: 46.6 us
  Pallas kernels  44.6 us (95%)
  local copies, waits for them, and re-layouts  1.98 us (4%)
    pallas_call x1, Pallas kernels, on_device(): pl.pallas_call(kernel, out_shape=jax.ShapeDtypeStruct((CH, 2 * OUT_LAT, N...  44.6 us
    reshape x1, local copies, waits for them, and re-layouts, on_device(): return result.reshape(CH, 2, OUT_LAT, NPC)  1.98 us

profile of v3, /device:TPU:1, one launch (start us, length us, event | category | flops | bytes accessed | tf_op | source)
XLA Modules:
  0.0 46.6 jit_solution(7892401186286366218)
XLA Ops:
  0.0 44.6 %shard_map.118 = f32[64,8,256]{2,1,0:T(8,128)} custom-call(s32[8,32]{1,0:T(8,128)} %bitcast.2, s32[8,32]{1,0:T(8,128)} %bitcast.3, s32[64]{0:T(128)} %parents_in.1, s32[64]{0:T(128)} %octants_in.1, f32[32,2,8,512]{3,2,1,0:T(8,128)} %patterns.1, f32[100,2,8,512]{3,2,1,0:T(8,128)} %operators.1, f32[32,2,8,512]{3,2,1,0:T(8,128)} %constant.12.clone.wave_x_in, ...), custom_call_target="tpu_custom_call" | custom-call | flops 1000000000 | bytes 6291456 | tf_op jit(solution)/shard_map/pallas_call | solution.py:296
  44.6 2.0 %reshape.3 = f32[64,2,4,256]{3,2,1,0:T(4,128)} reshape(f32[64,8,256]{2,1,0:T(8,128)} %shard_map.118) | data formatting | bytes 1048576 | tf_op jit(solution)/shard_map/reshape | solution.py:335

commit v4 on v3

--- a/solution.py
+++ b/solution.py
@@ -22,6 +22,11 @@
 PER = CH // MEM
 REACH = 6.0
 HALO_PARTS = 1
+PART = 8
+STEPS = sorted(
+    ((y, x, core) for y in range(4) for x in range(4) for core in range(2)),
+    key=lambda step: (step == (0, 0, 0), -min(step[0], 4 - step[0]) - min(step[1], 4 - step[1])),
+)
 
 
 def split(values):
@@ -83,7 +88,7 @@
     partners, factors, parents, octants,
     own, wide, ops, wave_x, wave_z, phi_high, phi_low, theta_high, theta_low,
     phase, translated, high, low, made, got, thin,
-    load_sem, halo_send, halo_recv, send_sem, recv_sem, back_send, back_recv,
+    load_sem, halo_send, halo_recv, send_sem, recv_sem, back_send, back_recv, turn,
 ):
     group = lax.axis_index("group")
     me = lax.axis_index("member")
@@ -112,11 +117,10 @@
     for one in loads:
         one.start()
 
-    def other(r):
-        y = lax.rem(me // 8 + r // 8, 4)
-        x = lax.rem(lax.rem(me // 2, 4) + lax.rem(r // 2, 4), 4)
-        c = lax.rem(me + r, 2)
-        return y * 8 + x * 2 + c
+    ys = [lax.rem(me // 8 + step, 4) * 8 for step in range(4)]
+    xs = [lax.rem(me // 2 + step, 4) * 2 for step in range(4)]
+    cores = [lax.rem(me + step, 2) for step in range(2)]
+    others = [ys[y] + xs[x] + cores[core] for y, x, core in STEPS]
 
     barrier = pltpu.get_barrier_semaphore()
 
@@ -128,9 +132,8 @@
     def _():
         pl.semaphore_signal(barrier, inc=1, device_id=(below, me), device_id_type=MESH)
 
-    @pl.loop(1, MEM)
-    def _(r):
-        pl.semaphore_signal(barrier, inc=1, device_id=(group, other(r)), device_id_type=MESH)
+    for member in others[: MEM - 1]:
+        pl.semaphore_signal(barrier, inc=1, device_id=(group, member), device_id_type=MESH)
 
     for one in loads[:2]:
         one.wait()
@@ -168,6 +171,10 @@
 
     pl.semaphore_wait(barrier, MEM - 1 + jnp.minimum(group, 1) + jnp.minimum(groups - 1 - group, 1))
 
+    @pl.when(lax.rem(me, 2) == 1)
+    def _():
+        pl.semaphore_wait(turn, 1)
+
     width = BAND // HALO_PARTS
 
     def up(n, to):
@@ -207,95 +214,94 @@
         @pl.when(has_above)
         def _():
             up(n, above).wait_send()
+
+        @pl.when(has_below)
+        def _():
+            down(n, below).wait_send()
+
+    @pl.when(lax.rem(me, 2) == 0)
+    def _():
+        pl.semaphore_signal(turn, inc=1, device_id=(group, ys[0] + xs[0] + cores[1]), device_id_type=MESH)
+
+    for n in range(HALO_PARTS):
+
+        @pl.when(has_above)
+        def _():
             down(n, above).wait_recv()
 
         @pl.when(has_below)
         def _():
-            down(n, below).wait_send()
             up(n, below).wait_recv()
 
     @pl.loop(0, 2 * BAND)
     def _(n):
         translate(jnp.where(n < BAND, n, n + CL - 2 * BAND), wide, group * CL - BAND)
 
-    def out_copy(r):
-        return pltpu.make_async_remote_copy(
-            src_ref=made.at[r],
-            dst_ref=got.at[me],
-            send_sem=send_sem.at[r],
-            recv_sem=recv_sem.at[r],
-            device_id=(group, other(r)),
-            device_id_type=MESH,
-        )
-
-    def shift_and_reduce(first, count):
-        @pl.loop(0, count)
-        def _(i):
-            member = other(lax.rem(first + i, MEM))
-            for k in range(PER):
-                child = member * PER + k
-                parent = translated[lax.rem(parents[child], CL)]
-                moved = times(parent, phase[octants[child]])
-                both = jnp.concatenate(moved, axis=0)
-                h, l = halves(both)
-                rows = pl.ds(pl.multiple_of((i * PER + k) * 2 * LAT, 2 * LAT), 2 * LAT)
-                high[rows, :] = h
-                low[rows, :] = l
-
-        total = count * PER * 2 * LAT
+    def shift_and_reduce(k, members):
+        for i, member in enumerate(members):
+            child = member * PER + k
+            parent = translated[lax.rem(parents[child], CL)]
+            moved = times(parent, phase[octants[child]])
+            both = jnp.concatenate(moved, axis=0)
+            h, l = halves(both)
+            rows = slice(i * 2 * LAT, (i + 1) * 2 * LAT)
+            high[rows, :] = h
+            low[rows, :] = l
+        total = len(members) * 2 * LAT
         h, l = high[:total, :], low[:total, :]
         result = dot(h, phi_high[...]) + dot(h, phi_low[...]) + dot(l, phi_high[...])
-        return result.reshape(count, PER, 2, LAT, NPC)
-
-    part = 8
-    for first in range(1, MEM, part):
-        block = shift_and_reduce(first, part)
-        left = min(part, MEM - first)
-        made[first : first + left] = block[:left]
-        if left < part:
-            got[me] = block[left]
-
-        @pl.loop(first, first + left)
-        def _(r):
-            out_copy(r).start()
-
-    @pl.loop(1, MEM)
-    def _(r):
-        out_copy(r).wait()
+        return result.reshape(len(members), 2, LAT, NPC)
+
+    def wait_for(blocks, sem):
+        pltpu.make_async_copy(blocks, blocks, sem).wait()
 
     for k in range(PER):
-        h, l = halves(got[:, k].reshape(MEM * 2 * LAT, NPC))
+        for first in range(0, MEM, PART):
+            members = others[first : first + PART]
+            block = shift_and_reduce(k, members)
+            made[k, first : first + PART] = block
+            for i, member in enumerate(members):
+                if first + i == MEM - 1:
+                    got[k, me] = block[i]
+                else:
+                    pltpu.make_async_remote_copy(
+                        src_ref=made.at[k, first + i],
+                        dst_ref=got.at[k, me],
+                        send_sem=send_sem.at[k],
+                        recv_sem=recv_sem.at[k],
+                        device_id=(group, member),
+                        device_id_type=MESH,
+                    ).start()
+
+    for k in range(PER):
+        wait_for(got.at[k, pl.ds(0, MEM - 1)], recv_sem.at[k])
+        h, l = halves(got[k].reshape(MEM * 2 * LAT, NPC))
         result = dot(theta_high[...], h) + dot(theta_low[...], h) + dot(theta_high[...], l)
-        thin[:, k] = result.reshape(MEM, 2 * OUT_LAT, NPC)
-
-    def back_copy(r):
-        return pltpu.make_async_remote_copy(
-            src_ref=thin.at[other(r)],
-            dst_ref=out.at[pl.ds(me * PER, PER)],
-            send_sem=back_send.at[r],
-            recv_sem=back_recv.at[r],
-            device_id=(group, other(r)),
-            device_id_type=MESH,
-        )
-
-    @pl.loop(1, MEM)
-    def _(r):
-        back_copy(r).start()
-
-    out[pl.ds(me * PER, PER)] = thin[me]
-
-    @pl.loop(1, MEM)
-    def _(r):
-        back_copy(r).wait()
+        thin[k] = result.reshape(thin.shape[1:])
+        for member in others[: MEM - 1]:
+            pltpu.make_async_remote_copy(
+                src_ref=thin.at[k, member],
+                dst_ref=out.at[me * PER + k],
+                send_sem=back_send.at[k],
+                recv_sem=back_recv.at[k],
+                device_id=(group, member),
+                device_id_type=MESH,
+            ).start()
+        out[me * PER + k] = thin[k, me]
+
+    for k in range(PER):
+        wait_for(made.at[k, pl.ds(0, MEM - 1)], send_sem.at[k])
+        wait_for(thin.at[k, pl.ds(0, MEM - 1)], back_send.at[k])
+        wait_for(thin.at[k, pl.ds(0, MEM - 1)], back_recv.at[k])
 
 
 def on_device(patterns, operators, partners, operator_index, child_parent, child_octant, *, constants):
     f32, bf16 = jnp.float32, jnp.bfloat16
     hbm = pl.BlockSpec(memory_space=pltpu.HBM)
     dma = pltpu.SemaphoreType.DMA
-    result = pl.pallas_call(
+    return pl.pallas_call(
         kernel,
-        out_shape=jax.ShapeDtypeStruct((CH, 2 * OUT_LAT, NPC), f32),
+        out_shape=jax.ShapeDtypeStruct((CH, 2, OUT_LAT, NPC), f32),
         in_specs=[hbm] * (6 + len(constants)),
         out_specs=pl.BlockSpec(memory_space=pltpu.VMEM),
         scratch_shapes=[
@@ -314,25 +320,25 @@
             pltpu.VMEM((2 * NTC, 2 * NT), bf16),
             pltpu.VMEM((8, 2, LAT, NP), f32),
             pltpu.VMEM((CL, 2, LAT, NP), f32),
-            pltpu.VMEM((256, NP), bf16),
-            pltpu.VMEM((256, NP), bf16),
-            pltpu.VMEM((MEM, PER, 2, LAT, NPC), f32),
-            pltpu.VMEM((MEM, PER, 2, LAT, NPC), f32),
-            pltpu.VMEM((MEM, PER, 2 * OUT_LAT, NPC), f32),
+            pltpu.VMEM((PART * 2 * LAT, NP), bf16),
+            pltpu.VMEM((PART * 2 * LAT, NP), bf16),
+            pltpu.VMEM((PER, MEM, 2, LAT, NPC), f32),
+            pltpu.VMEM((PER, MEM, 2, LAT, NPC), f32),
+            pltpu.VMEM((PER, MEM, 2, OUT_LAT, NPC), f32),
             dma((13,)),
             dma((2, HALO_PARTS)),
             dma((2, HALO_PARTS)),
-            dma((MEM,)),
-            dma((MEM,)),
-            dma((MEM,)),
-            dma((MEM,)),
+            dma((PER,)),
+            dma((PER,)),
+            dma((PER,)),
+            dma((PER,)),
+            pltpu.SemaphoreType.REGULAR,
         ],
         compiler_params=pltpu.CompilerParams(
             collective_id=0, has_side_effects=True, vmem_limit_bytes=60 * 2**20
         ),
         cost_estimate=pl.CostEstimate(flops=10**9, bytes_accessed=6 * 2**20, transcendentals=0),
     )(partners.T, operator_index.T, child_parent, child_octant, patterns, operators, *constants)
-    return result.reshape(CH, 2, OUT_LAT, NPC)
 
 
 def solution(mesh):

time: 47.1 us -> 38.6 us (0.82)
  Pallas kernels: 44.6 us -> 36.4 us
    pallas_call x1, Pallas kernels: 44.6 us -> 36.4 us  [on_device(): pl.pallas_call(kernel, out_shape=jax.ShapeDtypeStruct((CH, 2, OUT_LAT, NP...]
    reshape x1 -> x0, local copies, waits for them, and re-layouts: 1.98 us -> none  [on_device(): return result.reshape(CH, 2, OUT_LAT, NPC)]
    unnamed x0 -> x1, local copies, waits for them, and re-layouts: none -> 1.87 us
where the time goes in v4:
time: 38.6 us; the launch traced here: 38.3 us
  Pallas kernels  36.4 us (94%)
  local copies, waits for them, and re-layouts  1.87 us (5%)
    pallas_call x1, Pallas kernels, on_device(): pl.pallas_call(kernel, out_shape=jax.ShapeDtypeStruct((CH, 2, OUT_LAT, NP...  36.4 us
    unnamed x1, local copies, waits for them, and re-layouts  1.87 us

profile of v4, /device:TPU:1, one launch (start us, length us, event | category | flops | bytes accessed | tf_op | source)
XLA Modules:
  0.0 38.3 jit_solution(10951058050489467906)
XLA Ops:
  0.0 36.4 %shard_map.118 = f32[64,2,4,256]{3,2,1,0:T(4,128)} custom-call(s32[8,32]{1,0:T(8,128)} %bitcast.2, s32[8,32]{1,0:T(8,128)} %bitcast.3, s32[64]{0:T(128)} %parents_in.1, s32[64]{0:T(128)} %octants_in.1, f32[32,2,8,512]{3,2,1,0:T(8,128)} %patterns.1, f32[100,2,8,512]{3,2,1,0:T(8,128)} %operators.1, f32[32,2,8,512]{3,2,1,0:T(8,128)} %constant.12.clone.wave_x_in, ...), custom_call_target="tpu_custom_call" | custom-call | flops 1000000000 | bytes 6291456 | tf_op jit(solution)/shard_map/pallas_call | solution.py:302
  36.4 1.9 %copy.14 = f32[64,2,4,256]{3,2,1,0:T(4,128)} copy(f32[64,2,4,256]{3,2,1,0:T(4,128)} %shard_map.118) | data formatting | bytes 1048576

commit v5 on v4

--- a/solution.py
+++ b/solution.py
@@ -19,13 +19,15 @@
 MEM = 32
 LAT = NT // MEM
 OUT_LAT = NTC // MEM
-PER = CH // MEM
 REACH = 6.0
 HALO_PARTS = 1
+FIRST = 16
+CHIPS = 16
+ROUNDS = ((0, 1), (1, 2), (2, 4))
 PART = 8
 STEPS = sorted(
-    ((y, x, core) for y in range(4) for x in range(4) for core in range(2)),
-    key=lambda step: (step == (0, 0, 0), -min(step[0], 4 - step[0]) - min(step[1], 4 - step[1])),
+    ((y, x) for y in range(4) for x in range(4)),
+    key=lambda step: -min(step[0], 4 - step[0]) - min(step[1], 4 - step[1]),
 )
 
 
@@ -49,11 +51,7 @@
         (np.cos(np.outer(phi_coarse, modes)) * mode_weights) @ np.cos(np.outer(phi_fine, modes)).T
         + (np.sin(np.outer(phi_coarse, modes)) * mode_weights) @ np.sin(np.outer(phi_fine, modes)).T
     ) / NP
-    big = np.zeros((MEM, 2, OUT_LAT, MEM, 2, LAT))
-    blocks = theta.reshape(MEM, OUT_LAT, MEM, LAT)
-    for part in range(2):
-        big[:, part, :, :, part, :] = blocks
-    theta_high, theta_low = split(big.reshape(MEM * 2 * OUT_LAT, MEM * 2 * LAT))
+    theta_high, theta_low = split(theta)
     phi_high, phi_low = split(phi.T)
     arg = REACH * np.sin(theta_fine)[:, None] * np.cos(phi_fine)[None, :]
     wave_x = np.stack([np.cos(arg), np.sin(arg)]).reshape(2, MEM, LAT, NP).swapaxes(0, 1)
@@ -84,10 +82,10 @@
 
 def kernel(
     partners_in, factors_in, parents_in, octants_in, patterns, operators, wave_x_in, wave_z_in, phi_high_in, phi_low_in, theta_high_in, theta_low_in,
-    out,
+    out, rank,
     partners, factors, parents, octants,
     own, wide, ops, wave_x, wave_z, phi_high, phi_low, theta_high, theta_low,
-    phase, translated, high, low, made, got, thin,
+    order, order_held, phase, translated, high, low, made, got, thin,
     load_sem, halo_send, halo_recv, send_sem, recv_sem, back_send, back_recv, turn,
 ):
     group = lax.axis_index("group")
@@ -106,21 +104,22 @@
         load(3, factors_in, factors),
         load(4, patterns, own),
         load(5, operators, ops),
-        load(6, patterns, wide.at[pl.ds(BAND, CL)]),
-        load(7, parents_in, parents),
-        load(8, octants_in, octants),
-        load(9, phi_high_in, phi_high),
-        load(10, phi_low_in, phi_low),
+        load(6, parents_in, parents),
+        load(7, octants_in, octants),
+        load(8, phi_high_in, phi_high),
+        load(9, phi_low_in, phi_low),
+        load(10, patterns, wide.at[pl.ds(BAND, CL)]),
         load(11, theta_high_in, theta_high),
         load(12, theta_low_in, theta_low),
     ]
     for one in loads:
         one.start()
 
+    core = lax.rem(me, 2)
     ys = [lax.rem(me // 8 + step, 4) * 8 for step in range(4)]
     xs = [lax.rem(me // 2 + step, 4) * 2 for step in range(4)]
-    cores = [lax.rem(me + step, 2) for step in range(2)]
-    others = [ys[y] + xs[x] + cores[core] for y, x, core in STEPS]
+    chips = [ys[y] + xs[x] for y, x in STEPS]
+    others = [chip + part for chip in chips[:-1] for part in range(2)] + [chips[-1] + 1 - core]
 
     barrier = pltpu.get_barrier_semaphore()
 
@@ -132,7 +131,7 @@
     def _():
         pl.semaphore_signal(barrier, inc=1, device_id=(below, me), device_id_type=MESH)
 
-    for member in others[: MEM - 1]:
+    for member in others:
         pl.semaphore_signal(barrier, inc=1, device_id=(group, member), device_id_type=MESH)
 
     for one in loads[:2]:
@@ -169,11 +168,72 @@
     def _(cluster):
         translate(cluster, own, group * CL)
 
+    for one in loads[6:10]:
+        one.wait()
+    inner = []
+    for child in range(CH):
+        row = lax.rem(parents[child], CL)
+        inner.append(jnp.where((row >= BAND) & (row < CL - BAND), 1, 0))
+    count = sum(inner)
+    seen = jnp.int32(0)
+    lane = lax.broadcasted_iota(jnp.int32, (8, 128), 1)
+    child_of = jnp.zeros((8, 128), jnp.int32)
+    for child in range(CH):
+        place = jnp.where(inner[child] == 1, seen, count + child - seen)
+        rank[child] = place
+        child_of = jnp.where(lane == place, child, child_of)
+        seen = seen + inner[child]
+    order_held[...] = child_of
+    ordering = pltpu.make_async_copy(order_held, order, load_sem.at[0])
+    ordering.start()
+    ordering.wait()
+
+    def shift_and_reduce(begin, end, first, number):
+        rounds = end - begin
+        for n in range(number):
+            for k in range(rounds):
+                child = order[0, (begin + k) * FIRST + chips[first + n] // 2]
+                parent = translated[lax.rem(parents[child], CL)]
+                moved = times(parent, phase[octants[child]])
+                h, l = halves(jnp.concatenate(moved, axis=0))
+                at = (n * rounds + k) * 2 * LAT
+                high[at : at + 2 * LAT, :] = h
+                low[at : at + 2 * LAT, :] = l
+        total = number * rounds * 2 * LAT
+        h, l = high[:total, :], low[:total, :]
+        result = dot(h, phi_high[...]) + dot(h, phi_low[...]) + dot(l, phi_high[...])
+        result = result.reshape(number, rounds, 2, LAT, NPC)
+        for n in range(number):
+            made[begin:end, first + n] = result[n]
+
+    def send(index, chip, part):
+        begin, end = ROUNDS[index]
+        pltpu.make_async_remote_copy(
+            src_ref=made.at[pl.ds(begin, end - begin), chip, part],
+            dst_ref=got.at[pl.ds(begin, end - begin), me],
+            send_sem=send_sem.at[index],
+            recv_sem=recv_sem.at[index],
+            device_id=(group, chips[chip] + part),
+            device_id_type=MESH,
+        ).start()
+
+    def send_chips(index, first, number):
+        begin, end = ROUNDS[index]
+        for chip in range(first, first + number):
+            if chip < CHIPS - 1:
+                send(index, chip, 0)
+                send(index, chip, 1)
+            else:
+                send(index, chip, 1 - core)
+                got[begin:end, me] = made[begin:end, chip, core]
+
+    def wait_for(blocks, sem):
+        pltpu.make_async_copy(blocks, blocks, sem).wait()
+
+    for first in range(0, CHIPS, PART):
+        shift_and_reduce(*ROUNDS[0], first, PART)
+
     pl.semaphore_wait(barrier, MEM - 1 + jnp.minimum(group, 1) + jnp.minimum(groups - 1 - group, 1))
-
-    @pl.when(lax.rem(me, 2) == 1)
-    def _():
-        pl.semaphore_wait(turn, 1)
 
     width = BAND // HALO_PARTS
 
@@ -197,17 +257,29 @@
             device_id_type=MESH,
         )
 
-    for n in range(HALO_PARTS):
-
-        @pl.when(has_above)
-        def _():
-            up(n, above).start()
-
-        @pl.when(has_below)
-        def _():
-            down(n, below).start()
-
-    for one in loads[6:]:
+    def start_halo():
+        for n in range(HALO_PARTS):
+
+            @pl.when(has_above)
+            def _():
+                up(n, above).start()
+
+            @pl.when(has_below)
+            def _():
+                down(n, below).start()
+
+    @pl.when(core == 0)
+    def _():
+        start_halo()
+
+    send_chips(0, 0, CHIPS)
+
+    @pl.when(core == 1)
+    def _():
+        pl.semaphore_wait(turn, 1)
+        start_halo()
+
+    for one in loads[10:]:
         one.wait()
     for n in range(HALO_PARTS):
 
@@ -219,9 +291,9 @@
         def _():
             down(n, below).wait_send()
 
-    @pl.when(lax.rem(me, 2) == 0)
+    @pl.when(core == 0)
     def _():
-        pl.semaphore_signal(turn, inc=1, device_id=(group, ys[0] + xs[0] + cores[1]), device_id_type=MESH)
+        pl.semaphore_signal(turn, inc=1, device_id=(group, chips[-1] + 1), device_id_type=MESH)
 
     for n in range(HALO_PARTS):
 
@@ -237,73 +309,86 @@
     def _(n):
         translate(jnp.where(n < BAND, n, n + CL - 2 * BAND), wide, group * CL - BAND)
 
-    def shift_and_reduce(k, members):
-        for i, member in enumerate(members):
-            child = member * PER + k
-            parent = translated[lax.rem(parents[child], CL)]
-            moved = times(parent, phase[octants[child]])
-            both = jnp.concatenate(moved, axis=0)
-            h, l = halves(both)
-            rows = slice(i * 2 * LAT, (i + 1) * 2 * LAT)
-            high[rows, :] = h
-            low[rows, :] = l
-        total = len(members) * 2 * LAT
-        h, l = high[:total, :], low[:total, :]
-        result = dot(h, phi_high[...]) + dot(h, phi_low[...]) + dot(l, phi_high[...])
-        return result.reshape(len(members), 2, LAT, NPC)
-
-    def wait_for(blocks, sem):
-        pltpu.make_async_copy(blocks, blocks, sem).wait()
-
-    for k in range(PER):
-        for first in range(0, MEM, PART):
-            members = others[first : first + PART]
-            block = shift_and_reduce(k, members)
-            made[k, first : first + PART] = block
-            for i, member in enumerate(members):
-                if first + i == MEM - 1:
-                    got[k, me] = block[i]
-                else:
-                    pltpu.make_async_remote_copy(
-                        src_ref=made.at[k, first + i],
-                        dst_ref=got.at[k, me],
-                        send_sem=send_sem.at[k],
-                        recv_sem=recv_sem.at[k],
-                        device_id=(group, member),
-                        device_id_type=MESH,
-                    ).start()
-
-    for k in range(PER):
-        wait_for(got.at[k, pl.ds(0, MEM - 1)], recv_sem.at[k])
-        h, l = halves(got[k].reshape(MEM * 2 * LAT, NPC))
-        result = dot(theta_high[...], h) + dot(theta_low[...], h) + dot(theta_high[...], l)
-        thin[k] = result.reshape(thin.shape[1:])
-        for member in others[: MEM - 1]:
+    def mine(index):
+        begin, end = ROUNDS[index]
+        return pltpu.make_async_copy(
+            thin.at[pl.ds(begin, end - begin), me],
+            out.at[pl.ds(begin, end - begin), me // 2, core],
+            load_sem.at[1 + index],
+        )
+
+    def finish(index):
+        begin, end = ROUNDS[index]
+        rounds = pl.ds(begin, end - begin)
+        wait_for(got.at[rounds, pl.ds(0, MEM - 1)], recv_sem.at[index])
+        for k in range(begin, end):
+            h, l = halves(got[k].reshape(NT, NPC))
+            result = dot(theta_high[...], h) + dot(theta_low[...], h) + dot(theta_high[...], l)
+            thin[k] = result.reshape(MEM, OUT_LAT, NPC)
+        for member in others:
             pltpu.make_async_remote_copy(
-                src_ref=thin.at[k, member],
-                dst_ref=out.at[me * PER + k],
-                send_sem=back_send.at[k],
-                recv_sem=back_recv.at[k],
+                src_ref=thin.at[rounds, member],
+                dst_ref=out.at[rounds, me // 2, core],
+                send_sem=back_send.at[index],
+                recv_sem=back_recv.at[index],
                 device_id=(group, member),
                 device_id_type=MESH,
             ).start()
-        out[me * PER + k] = thin[k, me]
-
-    for k in range(PER):
-        wait_for(made.at[k, pl.ds(0, MEM - 1)], send_sem.at[k])
-        wait_for(thin.at[k, pl.ds(0, MEM - 1)], back_send.at[k])
-        wait_for(thin.at[k, pl.ds(0, MEM - 1)], back_recv.at[k])
+        mine(index).start()
+
+    for index in range(1, len(ROUNDS)):
+        begin, end = ROUNDS[index]
+        number = PART // (end - begin)
+        for first in range(0, CHIPS, number):
+            shift_and_reduce(begin, end, first, number)
+            send_chips(index, first, number)
+        finish(index - 1)
+    finish(len(ROUNDS) - 1)
+
+    for index, (begin, end) in enumerate(ROUNDS):
+        rounds = pl.ds(begin, end - begin)
+        mine(index).wait()
+        wait_for(got.at[rounds, pl.ds(0, MEM - 1)], send_sem.at[index])
+        wait_for(thin.at[rounds, pl.ds(0, MEM - 1)], back_send.at[index])
+        wait_for(thin.at[rounds, pl.ds(0, MEM - 1)], back_recv.at[index])
+
+
+def reorder(rank, ranked, out, held, ordered, load_sem, store_sem):
+    parts = 4
+    number = CH // parts
+
+    def load(part):
+        rows = pl.ds(part * number, number)
+        return pltpu.make_async_copy(ranked.at[rows], held.at[rows], load_sem.at[part])
+
+    def store(part):
+        rows = pl.ds(part * number, number)
+        return pltpu.make_async_copy(ordered.at[rows], out.at[rows], store_sem.at[part])
+
+    for part in range(parts):
+        load(part).start()
+    for part in range(parts):
+        load(part).wait()
+    for part in range(parts):
+        for child in range(part * number, (part + 1) * number):
+            ordered[child] = held[rank[child]]
+        store(part).start()
+    for part in range(parts):
+        store(part).wait()
 
 
 def on_device(patterns, operators, partners, operator_index, child_parent, child_octant, *, constants):
     f32, bf16 = jnp.float32, jnp.bfloat16
     hbm = pl.BlockSpec(memory_space=pltpu.HBM)
     dma = pltpu.SemaphoreType.DMA
-    return pl.pallas_call(
+    ranked, rank = pl.pallas_call(
         kernel,
-        out_shape=jax.ShapeDtypeStruct((CH, 2, OUT_LAT, NPC), f32),
+        out_shape=(
+            jax.ShapeDtypeStruct((CH // FIRST, CHIPS, 2, OUT_LAT, NPC), f32),
+            jax.ShapeDtypeStruct((CH,), jnp.int32),
+        ),
         in_specs=[hbm] * (6 + len(constants)),
-        out_specs=pl.BlockSpec(memory_space=pltpu.VMEM),
+        out_specs=(hbm, pl.BlockSpec(memory_space=pltpu.SMEM)),
         scratch_shapes=[
             pltpu.SMEM((NPART, CL), jnp.int32),
             pltpu.SMEM((NPART, CL), jnp.int32),
@@ -316,22 +401,24 @@
             pltpu.VMEM((2, LAT, 128), f32),
             pltpu.VMEM((NP, NPC), bf16),
             pltpu.VMEM((NP, NPC), bf16),
-            pltpu.VMEM((2 * NTC, 2 * NT), bf16),
-            pltpu.VMEM((2 * NTC, 2 * NT), bf16),
+            pltpu.VMEM((NTC, NT), bf16),
+            pltpu.VMEM((NTC, NT), bf16),
+            pltpu.SMEM((8, 128), jnp.int32),
+            pltpu.VMEM((8, 128), jnp.int32),
             pltpu.VMEM((8, 2, LAT, NP), f32),
             pltpu.VMEM((CL, 2, LAT, NP), f32),
             pltpu.VMEM((PART * 2 * LAT, NP), bf16),
             pltpu.VMEM((PART * 2 * LAT, NP), bf16),
-            pltpu.VMEM((PER, MEM, 2, LAT, NPC), f32),
-            pltpu.VMEM((PER, MEM, 2, LAT, NPC), f32),
-            pltpu.VMEM((PER, MEM, 2, OUT_LAT, NPC), f32),
+            pltpu.VMEM((CH // FIRST, CHIPS, 2, LAT, NPC), f32),
+            pltpu.VMEM((CH // FIRST, MEM, LAT, NPC), f32),
+            pltpu.VMEM((CH // FIRST, MEM, OUT_LAT, NPC), f32),
             dma((13,)),
             dma((2, HALO_PARTS)),
             dma((2, HALO_PARTS)),
-            dma((PER,)),
-            dma((PER,)),
-            dma((PER,)),
-            dma((PER,)),
+            dma((len(ROUNDS),)),
+            dma((len(ROUNDS),)),
+            dma((len(ROUNDS),)),
+            dma((len(ROUNDS),)),
             pltpu.SemaphoreType.REGULAR,
         ],
         compiler_params=pltpu.CompilerParams(
@@ -339,6 +426,15 @@
         ),
         cost_estimate=pl.CostEstimate(flops=10**9, bytes_accessed=6 * 2**20, transcendentals=0),
     )(partners.T, operator_index.T, child_parent, child_octant, patterns, operators, *constants)
+    shape = (CH, 2, OUT_LAT, NPC)
+    return pl.pallas_call(
+        reorder,
+        out_shape=jax.ShapeDtypeStruct(shape, f32),
+        in_specs=[pl.BlockSpec(memory_space=pltpu.SMEM), hbm],
+        out_specs=hbm,
+        scratch_shapes=[pltpu.VMEM(shape, f32), pltpu.VMEM(shape, f32), dma((4,)), dma((4,))],
+        compiler_params=pltpu.CompilerParams(vmem_limit_bytes=60 * 2**20),
+    )(rank, ranked.reshape(shape))
 
 
 def solution(mesh):

time: 38.6 us -> 39.2 us (1.016)
  Pallas kernels: 36.4 us -> 38.7 us
  local copies, waits for them, and re-layouts: 1.87 us -> 0 us
    pallas_call x1 -> x2, Pallas kernels: 36.4 us -> 38.7 us  [the longest x1 36 us: on_device(): pl.pallas_call(kernel, out_shape=(jax.ShapeDtypeStruct((CH // FIRST, CHIP...]
    unnamed x1 -> x0, local copies, waits for them, and re-layouts: 1.87 us -> none
where the time goes in v5:
time: 39.2 us; the launch traced here: 38.7 us
  Pallas kernels  38.7 us (99%)
    pallas_call x1, Pallas kernels, on_device(): pl.pallas_call(kernel, out_shape=(jax.ShapeDtypeStruct((CH // FIRST, CHIP...  36 us
    pallas_call x1, Pallas kernels, on_device(): pl.pallas_call(reorder, out_shape=jax.ShapeDtypeStruct(shape, f32), in_sp...  2.62 us

profile of v5, /device:TPU:1, one launch (start us, length us, event | category | flops | bytes accessed | tf_op | source)
XLA Modules:
  0.0 38.7 jit_solution(2458295158297648711)
XLA Ops:
  0.0 36.0 %shard_map.118 = (f32[4,16,2,4,256]{4,3,2,1,0:T(4,128)}, s32[64]{0:T(128)}) custom-call(s32[8,32]{1,0:T(8,128)} %bitcast.4, s32[8,32]{1,0:T(8,128)} %bitcast.5, s32[64]{0:T(128)} %parents_in.1, s32[64]{0:T(128)} %octants_in.1, f32[32,2,8,512]{3,2,1,0:T(8,128)} %patterns.1, f32[100,2,8,512]{3,2,1,0:T(8,128)} %operators.1, ...), custom_call_target="tpu_custom_call" | custom-call | flops 1000000000 | bytes 6291456 | tf_op jit(solution)/shard_map/pallas_call | solution.py:384
  36.1 2.6 %shard_map.119 = f32[64,2,4,256]{3,2,1,0:T(4,128)} custom-call(s32[64]{0:T(128)} %get-tuple-element.7.rank, f32[64,2,4,256]{3,2,1,0:T(4,128)} %bitcast.3), custom_call_target="tpu_custom_call" | custom-call | tf_op jit(solution)/shard_map/pallas_call | solution.py:430

commit v6 on v5

--- a/solution.py
+++ b/solution.py
@@ -23,7 +23,7 @@
 HALO_PARTS = 1
 FIRST = 16
 CHIPS = 16
-ROUNDS = ((0, 1), (1, 2), (2, 4))
+ROUNDS = ((0, 1), (1, 3), (3, 4))
 PART = 8
 STEPS = sorted(
     ((y, x) for y in range(4) for x in range(4)),
@@ -150,6 +150,45 @@
         full = times(xy, (z_real, sz * z_imag))
         phase[octant, 0], phase[octant, 1] = full
 
+    pl.semaphore_wait(barrier, MEM - 1 + jnp.minimum(group, 1) + jnp.minimum(groups - 1 - group, 1))
+
+    width = BAND // HALO_PARTS
+
+    def up(n, to):
+        return pltpu.make_async_remote_copy(
+            src_ref=patterns.at[pl.ds(CL - BAND + n * width, width)],
+            dst_ref=wide.at[pl.ds(n * width, width)],
+            send_sem=halo_send.at[0, n],
+            recv_sem=halo_recv.at[0, n],
+            device_id=(to, me),
+            device_id_type=MESH,
+        )
+
+    def down(n, to):
+        return pltpu.make_async_remote_copy(
+            src_ref=patterns.at[pl.ds(n * width, width)],
+            dst_ref=wide.at[pl.ds(CL + BAND + n * width, width)],
+            send_sem=halo_send.at[1, n],
+            recv_sem=halo_recv.at[1, n],
+            device_id=(to, me),
+            device_id_type=MESH,
+        )
+
+    def start_halo():
+        for n in range(HALO_PARTS):
+
+            @pl.when(has_above)
+            def _():
+                up(n, above).start()
+
+            @pl.when(has_below)
+            def _():
+                down(n, below).start()
+
+    @pl.when(core == 0)
+    def _():
+        start_halo()
+
     def translate(cluster, cells, first):
         real = jnp.zeros((LAT, NP), jnp.float32)
         imag = jnp.zeros((LAT, NP), jnp.float32)
@@ -167,6 +206,17 @@
     @pl.loop(BAND, CL - BAND)
     def _(cluster):
         translate(cluster, own, group * CL)
+
+    def wait_sent():
+        for n in range(HALO_PARTS):
+
+            @pl.when(has_above)
+            def _():
+                up(n, above).wait_send()
+
+            @pl.when(has_below)
+            def _():
+                down(n, below).wait_send()
 
     for one in loads[6:10]:
         one.wait()
@@ -233,46 +283,12 @@
     for first in range(0, CHIPS, PART):
         shift_and_reduce(*ROUNDS[0], first, PART)
 
-    pl.semaphore_wait(barrier, MEM - 1 + jnp.minimum(group, 1) + jnp.minimum(groups - 1 - group, 1))
-
-    width = BAND // HALO_PARTS
-
-    def up(n, to):
-        return pltpu.make_async_remote_copy(
-            src_ref=patterns.at[pl.ds(CL - BAND + n * width, width)],
-            dst_ref=wide.at[pl.ds(n * width, width)],
-            send_sem=halo_send.at[0, n],
-            recv_sem=halo_recv.at[0, n],
-            device_id=(to, me),
-            device_id_type=MESH,
-        )
-
-    def down(n, to):
-        return pltpu.make_async_remote_copy(
-            src_ref=patterns.at[pl.ds(n * width, width)],
-            dst_ref=wide.at[pl.ds(CL + BAND + n * width, width)],
-            send_sem=halo_send.at[1, n],
-            recv_sem=halo_recv.at[1, n],
-            device_id=(to, me),
-            device_id_type=MESH,
-        )
-
-    def start_halo():
-        for n in range(HALO_PARTS):
-
-            @pl.when(has_above)
-            def _():
-                up(n, above).start()
-
-            @pl.when(has_below)
-            def _():
-                down(n, below).start()
+    send_chips(0, 0, CHIPS)
 
     @pl.when(core == 0)
     def _():
-        start_halo()
-
-    send_chips(0, 0, CHIPS)
+        wait_sent()
+        pl.semaphore_signal(turn, inc=1, device_id=(group, chips[-1] + 1), device_id_type=MESH)
 
     @pl.when(core == 1)
     def _():
@@ -281,33 +297,6 @@
 
     for one in loads[10:]:
         one.wait()
-    for n in range(HALO_PARTS):
-
-        @pl.when(has_above)
-        def _():
-            up(n, above).wait_send()
-
-        @pl.when(has_below)
-        def _():
-            down(n, below).wait_send()
-
-    @pl.when(core == 0)
-    def _():
-        pl.semaphore_signal(turn, inc=1, device_id=(group, chips[-1] + 1), device_id_type=MESH)
-
-    for n in range(HALO_PARTS):
-
-        @pl.when(has_above)
-        def _():
-            down(n, above).wait_recv()
-
-        @pl.when(has_below)
-        def _():
-            up(n, below).wait_recv()
-
-    @pl.loop(0, 2 * BAND)
-    def _(n):
-        translate(jnp.where(n < BAND, n, n + CL - 2 * BAND), wide, group * CL - BAND)
 
     def mine(index):
         begin, end = ROUNDS[index]
@@ -336,14 +325,43 @@
             ).start()
         mine(index).start()
 
+    @pl.when(core == 1)
+    def _():
+        finish(0)
+
+    for n in range(HALO_PARTS):
+
+        @pl.when(has_above)
+        def _():
+            down(n, above).wait_recv()
+
+        @pl.when(has_below)
+        def _():
+            up(n, below).wait_recv()
+
+    @pl.loop(0, 2 * BAND)
+    def _(n):
+        translate(jnp.where(n < BAND, n, n + CL - 2 * BAND), wide, group * CL - BAND)
+
     for index in range(1, len(ROUNDS)):
         begin, end = ROUNDS[index]
         number = PART // (end - begin)
         for first in range(0, CHIPS, number):
             shift_and_reduce(begin, end, first, number)
             send_chips(index, first, number)
-        finish(index - 1)
+        if index == 1:
+
+            @pl.when(core == 0)
+            def _():
+                finish(0)
+
+        else:
+            finish(index - 1)
     finish(len(ROUNDS) - 1)
+
+    @pl.when(core == 1)
+    def _():
+        wait_sent()
 
     for index, (begin, end) in enumerate(ROUNDS):
         rounds = pl.ds(begin, end - begin)
@@ -353,7 +371,7 @@
         wait_for(thin.at[rounds, pl.ds(0, MEM - 1)], back_recv.at[index])
 
 
-def reorder(rank, ranked, out, held, ordered, load_sem, store_sem):
+def reorder(rank_in, ranked, out, rank, held, ordered, load_sem, store_sem):
     parts = 4
     number = CH // parts
 
@@ -365,8 +383,11 @@
         rows = pl.ds(part * number, number)
         return pltpu.make_async_copy(ordered.at[rows], out.at[rows], store_sem.at[part])
 
+    ranks = pltpu.make_async_copy(rank_in, rank, load_sem.at[parts])
+    ranks.start()
     for part in range(parts):
         load(part).start()
+    ranks.wait()
     for part in range(parts):
         load(part).wait()
     for part in range(parts):
@@ -430,9 +451,9 @@
     return pl.pallas_call(
         reorder,
         out_shape=jax.ShapeDtypeStruct(shape, f32),
-        in_specs=[pl.BlockSpec(memory_space=pltpu.SMEM), hbm],
+        in_specs=[hbm, hbm],
         out_specs=hbm,
-        scratch_shapes=[pltpu.VMEM(shape, f32), pltpu.VMEM(shape, f32), dma((4,)), dma((4,))],
+        scratch_shapes=[pltpu.SMEM((CH,), jnp.int32), pltpu.VMEM(shape, f32), pltpu.VMEM(shape, f32), dma((5,)), dma((4,))],
         compiler_params=pltpu.CompilerParams(vmem_limit_bytes=60 * 2**20),
     )(rank, ranked.reshape(shape))
 

time: 39.2 us -> 36.8 us (0.939)
  Pallas kernels: 38.7 us -> 36.6 us
    pallas_call x1, Pallas kernels: 36 us -> 34.7 us  [on_device(): pl.pallas_call(kernel, out_shape=(jax.ShapeDtypeStruct((CH // FIRST, CHIP...]
    pallas_call x1, Pallas kernels: 2.62 us -> 1.97 us  [on_device(): pl.pallas_call(reorder, out_shape=jax.ShapeDtypeStruct(shape, f32), in_sp...]
where the time goes in v6:
time: 36.8 us; the launch traced here: 36.6 us
  Pallas kernels  36.6 us (99%)
    pallas_call x1, Pallas kernels, on_device(): pl.pallas_call(kernel, out_shape=(jax.ShapeDtypeStruct((CH // FIRST, CHIP...  34.7 us
    pallas_call x1, Pallas kernels, on_device(): pl.pallas_call(reorder, out_shape=jax.ShapeDtypeStruct(shape, f32), in_sp...  1.97 us

profile of v6, /device:TPU:1, one launch (start us, length us, event | category | flops | bytes accessed | tf_op | source)
XLA Modules:
  0.0 36.6 jit_solution(3322575133790833971)
XLA Ops:
  0.0 34.7 %shard_map.118 = (f32[4,16,2,4,256]{4,3,2,1,0:T(4,128)}, s32[64]{0:T(128)}) custom-call(s32[8,32]{1,0:T(8,128)} %bitcast.4, s32[8,32]{1,0:T(8,128)} %bitcast.5, s32[64]{0:T(128)} %parents_in.1, s32[64]{0:T(128)} %octants_in.1, f32[32,2,8,512]{3,2,1,0:T(8,128)} %patterns.1, f32[100,2,8,512]{3,2,1,0:T(8,128)} %operators.1, ...), custom_call_target="tpu_custom_call" | custom-call | flops 1000000000 | bytes 6291456 | tf_op jit(solution)/shard_map/pallas_call | solution.py:405
  34.7 2.0 %shard_map.119 = f32[64,2,4,256]{3,2,1,0:T(4,128)} custom-call(s32[64]{0:T(128)} %get-tuple-element.7.rank_in, f32[64,2,4,256]{3,2,1,0:T(4,128)} %bitcast.3), custom_call_target="tpu_custom_call" | custom-call | tf_op jit(solution)/shard_map/pallas_call | solution.py:451

commit v7 on v6

--- a/solution.py
+++ b/solution.py
@@ -371,28 +371,20 @@
         wait_for(thin.at[rounds, pl.ds(0, MEM - 1)], back_recv.at[index])
 
 
-def reorder(rank_in, ranked, out, rank, held, ordered, load_sem, store_sem):
+def reorder(rank_in, ranked, out, rank, ordered, load_sem, store_sem):
+    ranks = pltpu.make_async_copy(rank_in, rank, load_sem)
+    ranks.start()
     parts = 4
     number = CH // parts
-
-    def load(part):
-        rows = pl.ds(part * number, number)
-        return pltpu.make_async_copy(ranked.at[rows], held.at[rows], load_sem.at[part])
 
     def store(part):
         rows = pl.ds(part * number, number)
         return pltpu.make_async_copy(ordered.at[rows], out.at[rows], store_sem.at[part])
 
-    ranks = pltpu.make_async_copy(rank_in, rank, load_sem.at[parts])
-    ranks.start()
-    for part in range(parts):
-        load(part).start()
     ranks.wait()
     for part in range(parts):
-        load(part).wait()
-    for part in range(parts):
         for child in range(part * number, (part + 1) * number):
-            ordered[child] = held[rank[child]]
+            ordered[child] = ranked[rank[child]]
         store(part).start()
     for part in range(parts):
         store(part).wait()
@@ -402,14 +394,15 @@
     f32, bf16 = jnp.float32, jnp.bfloat16
     hbm = pl.BlockSpec(memory_space=pltpu.HBM)
     dma = pltpu.SemaphoreType.DMA
+    operands = (partners.T, operator_index.T, child_parent, child_octant, patterns, operators, *constants)
     ranked, rank = pl.pallas_call(
         kernel,
         out_shape=(
-            jax.ShapeDtypeStruct((CH // FIRST, CHIPS, 2, OUT_LAT, NPC), f32),
+            pltpu.VMEM((CH // FIRST, CHIPS, 2, OUT_LAT, NPC), f32),
             jax.ShapeDtypeStruct((CH,), jnp.int32),
         ),
         in_specs=[hbm] * (6 + len(constants)),
-        out_specs=(hbm, pl.BlockSpec(memory_space=pltpu.SMEM)),
+        out_specs=(pl.BlockSpec(memory_space=pltpu.VMEM), pl.BlockSpec(memory_space=pltpu.SMEM)),
         scratch_shapes=[
             pltpu.SMEM((NPART, CL), jnp.int32),
             pltpu.SMEM((NPART, CL), jnp.int32),
@@ -443,18 +436,18 @@
             pltpu.SemaphoreType.REGULAR,
         ],
         compiler_params=pltpu.CompilerParams(
-            collective_id=0, has_side_effects=True, vmem_limit_bytes=60 * 2**20
+            collective_id=0, has_side_effects=True, vmem_limit_bytes=40 * 2**20
         ),
         cost_estimate=pl.CostEstimate(flops=10**9, bytes_accessed=6 * 2**20, transcendentals=0),
-    )(partners.T, operator_index.T, child_parent, child_octant, patterns, operators, *constants)
+    )(*(pltpu.with_memory_space_constraint(jnp.asarray(x), pltpu.HBM) for x in operands))
     shape = (CH, 2, OUT_LAT, NPC)
     return pl.pallas_call(
         reorder,
         out_shape=jax.ShapeDtypeStruct(shape, f32),
-        in_specs=[hbm, hbm],
+        in_specs=[hbm, pl.BlockSpec(memory_space=pltpu.VMEM)],
         out_specs=hbm,
-        scratch_shapes=[pltpu.SMEM((CH,), jnp.int32), pltpu.VMEM(shape, f32), pltpu.VMEM(shape, f32), dma((5,)), dma((4,))],
-        compiler_params=pltpu.CompilerParams(vmem_limit_bytes=60 * 2**20),
+        scratch_shapes=[pltpu.SMEM((CH,), jnp.int32), pltpu.VMEM(shape, f32), dma(()), dma((4,))],
+        compiler_params=pltpu.CompilerParams(vmem_limit_bytes=40 * 2**20),
     )(rank, ranked.reshape(shape))
 
 

time: 36.8 us -> 36.2 us (0.984)
  Pallas kernels: 36.6 us -> 36 us
    pallas_call x1, Pallas kernels: 1.97 us -> 1.38 us  [on_device(): pl.pallas_call(reorder, out_shape=jax.ShapeDtypeStruct(shape, f32), in_sp...]
where the time goes in v7:
time: 36.2 us; the launch traced here: 36 us
  Pallas kernels  36 us (99%)
    pallas_call x1, Pallas kernels, on_device(): pl.pallas_call(kernel, out_shape=(pltpu.VMEM((CH // FIRST, CHIPS, 2, OUT_...  34.6 us
    pallas_call x1, Pallas kernels, on_device(): pl.pallas_call(reorder, out_shape=jax.ShapeDtypeStruct(shape, f32), in_sp...  1.38 us

profile of v7, /device:TPU:1, one launch (start us, length us, event | category | flops | bytes accessed | tf_op | source)
XLA Modules:
  0.0 36.0 jit_solution(11838185112037570668)
XLA Ops:
  0.0 34.6 %shard_map.118 = (f32[4,16,2,4,256]{4,3,2,1,0:T(4,128)S(1)}, s32[64]{0:T(128)S(1)}) custom-call(s32[8,32]{1,0:T(8,128)} %bitcast.4, s32[8,32]{1,0:T(8,128)} %bitcast.5, s32[64]{0:T(128)} %parents_in.1, s32[64]{0:T(128)} %octants_in.1, f32[32,2,8,512]{3,2,1,0:T(8,128)} %patterns.1, f32[100,2,8,512]{3,2,1,0:T(8,128)} %operators.1, ...), custom_call_target="tpu_custom_call" | custom-call | flops 1000000000 | bytes 6291456 | tf_op jit(solution)/shard_map/pallas_call | solution.py:398
  34.6 1.4 %shard_map.119 = f32[64,2,4,256]{3,2,1,0:T(4,128)} custom-call(s32[64]{0:T(128)S(1)} %get-tuple-element.7.rank_in, f32[64,2,4,256]{3,2,1,0:T(4,128)S(1)} %bitcast.3), custom_call_target="tpu_custom_call" | custom-call | tf_op jit(solution)/shard_map/pallas_call | solution.py:444

commit v8 on v7

--- a/solution.py
+++ b/solution.py
@@ -23,7 +23,7 @@
 HALO_PARTS = 1
 FIRST = 16
 CHIPS = 16
-ROUNDS = ((0, 1), (1, 3), (3, 4))
+ROUNDS = ((0, 1), (1, 2), (2, 3), (3, 4))
 PART = 8
 STEPS = sorted(
     ((y, x) for y in range(4) for x in range(4)),
@@ -349,15 +349,12 @@
         for first in range(0, CHIPS, number):
             shift_and_reduce(begin, end, first, number)
             send_chips(index, first, number)
-        if index == 1:
-
-            @pl.when(core == 0)
-            def _():
-                finish(0)
-
-        else:
-            finish(index - 1)
-    finish(len(ROUNDS) - 1)
+    @pl.when(core == 0)
+    def _():
+        finish(0)
+
+    for index in range(1, len(ROUNDS)):
+        finish(index)
 
     @pl.when(core == 1)
     def _():

time: 36.2 us -> 35.1 us (0.970)
  Pallas kernels: 36 us -> 34.6 us
    pallas_call x1, Pallas kernels: 34.6 us -> 33.3 us  [on_device(): pl.pallas_call(kernel, out_shape=(pltpu.VMEM((CH // FIRST, CHIPS, 2, OUT_...]
where the time goes in v8:
time: 35.1 us; the launch traced here: 34.7 us
  Pallas kernels  34.6 us (99%)
    pallas_call x1, Pallas kernels, on_device(): pl.pallas_call(kernel, out_shape=(pltpu.VMEM((CH // FIRST, CHIPS, 2, OUT_...  33.3 us
    pallas_call x1, Pallas kernels, on_device(): pl.pallas_call(reorder, out_shape=jax.ShapeDtypeStruct(shape, f32), in_sp...  1.38 us

profile of v8, /device:TPU:1, one launch (start us, length us, event | category | flops | bytes accessed | tf_op | source)
XLA Modules:
  0.0 34.7 jit_solution(15606603134586982900)
XLA Ops:
  0.0 33.3 %shard_map.118 = (f32[4,16,2,4,256]{4,3,2,1,0:T(4,128)S(1)}, s32[64]{0:T(128)S(1)}) custom-call(s32[8,32]{1,0:T(8,128)} %bitcast.4, s32[8,32]{1,0:T(8,128)} %bitcast.5, s32[64]{0:T(128)} %parents_in.1, s32[64]{0:T(128)} %octants_in.1, f32[32,2,8,512]{3,2,1,0:T(8,128)} %patterns.1, f32[100,2,8,512]{3,2,1,0:T(8,128)} %operators.1, ...), custom_call_target="tpu_custom_call" | custom-call | flops 1000000000 | bytes 6291456 | tf_op jit(solution)/shard_map/pallas_call | solution.py:395
  33.3 1.4 %shard_map.119 = f32[64,2,4,256]{3,2,1,0:T(4,128)} custom-call(s32[64]{0:T(128)S(1)} %get-tuple-element.7.rank_in, f32[64,2,4,256]{3,2,1,0:T(4,128)S(1)} %bitcast.3), custom_call_target="tpu_custom_call" | custom-call | tf_op jit(solution)/shard_map/pallas_call | solution.py:441

commit v9 on v8

--- a/solution.py
+++ b/solution.py
@@ -116,6 +116,7 @@
         one.start()
 
     core = lax.rem(me, 2)
+    late = lax.rem(me + me // 8 + me // 2, 2)
     ys = [lax.rem(me // 8 + step, 4) * 8 for step in range(4)]
     xs = [lax.rem(me // 2 + step, 4) * 2 for step in range(4)]
     chips = [ys[y] + xs[x] for y, x in STEPS]
@@ -185,7 +186,7 @@
             def _():
                 down(n, below).start()
 
-    @pl.when(core == 0)
+    @pl.when(late == 0)
     def _():
         start_halo()
 
@@ -285,12 +286,12 @@
 
     send_chips(0, 0, CHIPS)
 
-    @pl.when(core == 0)
+    @pl.when(late == 0)
     def _():
         wait_sent()
-        pl.semaphore_signal(turn, inc=1, device_id=(group, chips[-1] + 1), device_id_type=MESH)
-
-    @pl.when(core == 1)
+        pl.semaphore_signal(turn, inc=1, device_id=(group, chips[-1] + 1 - core), device_id_type=MESH)
+
+    @pl.when(late == 1)
     def _():
         pl.semaphore_wait(turn, 1)
         start_halo()
@@ -325,7 +326,7 @@
             ).start()
         mine(index).start()
 
-    @pl.when(core == 1)
+    @pl.when(late == 1)
     def _():
         finish(0)
 
@@ -349,14 +350,14 @@
         for first in range(0, CHIPS, number):
             shift_and_reduce(begin, end, first, number)
             send_chips(index, first, number)
-    @pl.when(core == 0)
+    @pl.when(late == 0)
     def _():
         finish(0)
 
     for index in range(1, len(ROUNDS)):
         finish(index)
 
-    @pl.when(core == 1)
+    @pl.when(late == 1)
     def _():
         wait_sent()
 

time: 35.1 us -> 34.8 us (level)
  no operation moved by 1% of the time
where the time goes in v9:
time: 34.8 us; the launch traced here: 34.4 us
  Pallas kernels  34.4 us (99%)
    pallas_call x1, Pallas kernels, on_device(): pl.pallas_call(kernel, out_shape=(pltpu.VMEM((CH // FIRST, CHIPS, 2, OUT_...  33 us
    pallas_call x1, Pallas kernels, on_device(): pl.pallas_call(reorder, out_shape=jax.ShapeDtypeStruct(shape, f32), in_sp...  1.38 us

profile of v9, /device:TPU:1, one launch (start us, length us, event | category | flops | bytes accessed | tf_op | source)
XLA Modules:
  0.0 34.4 jit_solution(1644440704472930043)
XLA Ops:
  0.0 33.0 %shard_map.118 = (f32[4,16,2,4,256]{4,3,2,1,0:T(4,128)S(1)}, s32[64]{0:T(128)S(1)}) custom-call(s32[8,32]{1,0:T(8,128)} %bitcast.4, s32[8,32]{1,0:T(8,128)} %bitcast.5, s32[64]{0:T(128)} %parents_in.1, s32[64]{0:T(128)} %octants_in.1, f32[32,2,8,512]{3,2,1,0:T(8,128)} %patterns.1, f32[100,2,8,512]{3,2,1,0:T(8,128)} %operators.1, ...), custom_call_target="tpu_custom_call" | custom-call | flops 1000000000 | bytes 6291456 | tf_op jit(solution)/shard_map/pallas_call | solution.py:396
  33.0 1.4 %shard_map.119 = f32[64,2,4,256]{3,2,1,0:T(4,128)} custom-call(s32[64]{0:T(128)S(1)} %get-tuple-element.7.rank_in, f32[64,2,4,256]{3,2,1,0:T(4,128)S(1)} %bitcast.3), custom_call_target="tpu_custom_call" | custom-call | tf_op jit(solution)/shard_map/pallas_call | solution.py:442

commit v10 on v8

--- a/solution.py
+++ b/solution.py
@@ -349,9 +349,11 @@
         for first in range(0, CHIPS, number):
             shift_and_reduce(begin, end, first, number)
             send_chips(index, first, number)
-    @pl.when(core == 0)
-    def _():
-        finish(0)
+        if index == 2:
+
+            @pl.when(core == 0)
+            def _():
+                finish(0)
 
     for index in range(1, len(ROUNDS)):
         finish(index)

time: 35.1 us -> 35.1 us (level)
  no operation moved by 1% of the time
where the time goes in v10:
time: 35.1 us; the launch traced here: 34.7 us
  Pallas kernels  34.6 us (99%)
    pallas_call x1, Pallas kernels, on_device(): pl.pallas_call(kernel, out_shape=(pltpu.VMEM((CH // FIRST, CHIPS, 2, OUT_...  33.3 us
    pallas_call x1, Pallas kernels, on_device(): pl.pallas_call(reorder, out_shape=jax.ShapeDtypeStruct(shape, f32), in_sp...  1.38 us

profile of v10, /device:TPU:1, one launch (start us, length us, event | category | flops | bytes accessed | tf_op | source)
XLA Modules:
  0.0 34.7 jit_solution(5947411344130545083)
XLA Ops:
  0.0 33.3 %shard_map.118 = (f32[4,16,2,4,256]{4,3,2,1,0:T(4,128)S(1)}, s32[64]{0:T(128)S(1)}) custom-call(s32[8,32]{1,0:T(8,128)} %bitcast.4, s32[8,32]{1,0:T(8,128)} %bitcast.5, s32[64]{0:T(128)} %parents_in.1, s32[64]{0:T(128)} %octants_in.1, f32[32,2,8,512]{3,2,1,0:T(8,128)} %patterns.1, f32[100,2,8,512]{3,2,1,0:T(8,128)} %operators.1, ...), custom_call_target="tpu_custom_call" | custom-call | flops 1000000000 | bytes 6291456 | tf_op jit(solution)/shard_map/pallas_call | solution.py:397
  33.3 1.4 %shard_map.119 = f32[64,2,4,256]{3,2,1,0:T(4,128)} custom-call(s32[64]{0:T(128)S(1)} %get-tuple-element.7.rank_in, f32[64,2,4,256]{3,2,1,0:T(4,128)S(1)} %bitcast.3), custom_call_target="tpu_custom_call" | custom-call | tf_op jit(solution)/shard_map/pallas_call | solution.py:443
